TPU v7x, 128 devices: a whole 4x4x4 slice. The times are simulated.
128 devices in a mesh: row: 8 (over x_lo, y), col: 16 (over z, x_hi, core).
Axes of the slice: x: 4 (x_hi: 2, x_lo: 2; x = x_hi * 2 + x_lo), y: 4, z: 4, core: 2. Of those that a mesh axis runs over, the one named last changes fastest.
Arguments:
- hidden: bfloat16 [2048, 36864], P('col', 'row'), may hold values from -6 to 6
- weight: bfloat16 [36864, 4608], P('row', 'col'), may hold values from -0.03125 to 0.03125
- scale_exp: int32 [384, 48], P('row', 'col'), may hold values from -14 to -8
- teacher: bfloat16 [2048, 4608], P(('row', 'col')), may hold values from -6 to 6
Outputs:
- student_out: bfloat16 [2048, 4608], P('row', 'col')
- weight_grad: bfloat16 [36864, 4608], P('row', 'col')
Inputs may be any that keep to these rules, and one draw needn't show every extreme that they name: `scale_exp`: integer exponents.
All inputs are finite; a program needn't handle non-finite values.
Results may differ from a plain program's by a relative error of at most 0.0065.
Values may be sent and summed in bfloat16 or wider, within the bound.
A program may use at most 128 MiB of HBM per device.

v0:
```python
import math

import jax
import jax.numpy as jnp
from jax import lax
from jax.sharding import PartitionSpec as P


def quantize(weight, scale_exp):
    tile_rows = weight.shape[0] // scale_exp.shape[0]
    step_size = jnp.left_shift(jnp.int32(1), scale_exp + 14).astype(jnp.float32) * 2.0 ** (-14)
    inverse = jnp.left_shift(jnp.int32(1), -8 - scale_exp).astype(jnp.float32) * 256.0
    step_cols = jnp.repeat(step_size, tile_rows, axis=1)
    inverse_cols = jnp.repeat(inverse, tile_rows, axis=1)
    grouped = weight.astype(jnp.float32).reshape(scale_exp.shape[0], tile_rows, weight.shape[1])
    levels = jnp.floor(grouped * inverse_cols[:, None, :] + 0.5)
    keep_mask = (jnp.abs(levels) <= 127.0).astype(jnp.float32).reshape(weight.shape)
    quantized = (
        (jnp.clip(levels, -127.0, 127.0) * step_cols[:, None, :])
        .reshape(weight.shape)
        .astype(jnp.bfloat16)
    )
    return (quantized, keep_mask)


def local(hidden, weight, scale_exp, teacher):
    quantized, keep_mask = quantize(weight, scale_exp)
    total_tokens = hidden.shape[0] * lax.axis_size("col")
    factor = 1.0 / math.sqrt(total_tokens)
    gathered = lax.all_gather(hidden, "col", axis=0, tiled=True)
    partial_out = jnp.dot(gathered, quantized, preferred_element_type=jnp.float32)
    columns = lax.all_to_all(teacher, "col", split_axis=1, concat_axis=0, tiled=True)
    student_all = lax.psum(partial_out, "row")
    target = lax.all_gather(columns, "row", axis=0, tiled=True)
    grad_out = ((student_all - target.astype(jnp.float32)) * factor).astype(jnp.bfloat16)
    share_rows = student_all.shape[0] // lax.axis_size("row")
    own_rows = lax.dynamic_slice_in_dim(
        student_all, lax.axis_index("row") * share_rows, share_rows, 0
    )
    student_out = own_rows.astype(jnp.bfloat16)
    product = lax.dot_general(
        gathered, grad_out, (((0,), (0,)), ((), ())), preferred_element_type=jnp.float32
    )
    return (student_out, (product * keep_mask).astype(jnp.bfloat16))


def solution(mesh):
    placed = (P("col", "row"), P("row", "col"), P("row", "col"), P(("row", "col"), None))
    return jax.shard_map(
        local,
        mesh=mesh,
        in_specs=placed,
        out_specs=(P("row", "col"), P("row", "col")),
        check_vma=False,
    )
```

profile of v0, /device:TPU:0, one launch (start us, length us, event | category | flops | bytes accessed | tf_op | source)
XLA Modules:
  0.0 286.9 jit_solution(18331329995193691046)
XLA Ops:
  7.2 0.0 all-gather.3.cloned.1.call-start
  7.2 0.7 all-gather.3.cloned.1.call-update
  7.9 0.0 all-reduce.2.cloned.1.call-start
  7.9 0.7 convert_multiply_fusion.1
  8.6 4.2 %mul.54 = f32[48,96,288]{1,0,2:T(8,128)} broadcast(f32[48,288]{0,1:T(8,128)S(1)} %bitcast.20), dimensions={0,2} | broadcast | bytes 5363712 | tf_op jit(solution)/shard_map/mul | solution.py:16
  12.8 8.3 %mul.55 = f32[4608,288]{0,1:T(8,128)} reshape(f32[48,96,288]{1,0,2:T(8,128)} %mul.54) | data formatting | bytes 10616832 | tf_op jit(solution)/shard_map/mul | solution.py:16
  21.1 4.2 %mul.60 = f32[48,96,288]{1,0,2:T(8,128)} broadcast(f32[48,288]{0,1:T(8,128)S(1)} %bitcast.21), dimensions={0,2} | broadcast | bytes 5363712 | tf_op jit(solution)/shard_map/mul | solution.py:19
  25.3 0.0 copy-start.1
  25.3 8.5 %mul.61 = f32[4608,288]{0,1:T(8,128)} reshape(f32[48,96,288]{1,0,2:T(8,128)} %mul.60) | data formatting | bytes 10616832 | tf_op jit(solution)/shard_map/mul | solution.py:19
  33.8 0.0 copy-start
  33.8 98.2 %all-gather.3.cloned.1.call-done = bf16[2048,4608]{1,0:T(8,128)(2,1)} async-done(((bf16[128,4608]{1,0:T(8,128)(2,1)}), bf16[2048,4608]{1,0:T(8,128)(2,1)}) %all-gather.3.cloned.1.call-update) | async-done | bytes 18874384 | tf_op jit(solution)/shard_map/all_gather | solution.py:30
  131.9 0.0 copy-done.1
  132.0 13.6 %convolution_bitcast_fusion.1 = f32[2048,288]{0,1:T(8,128)} fusion(bf16[2048,4608]{1,0:T(8,128)(2,1)} %all-gather.3.cloned.1.call-done, f32[4608,288]{0,1:T(8,128)} %mul.61, f32[4608,288]{0,1:T(8,128)} %mul.55, bf16[4608,288]{0,1:T(8,128)(2,1)S(1)} %copy-done.1), kind=kOutput, calls=%fused_computation.6 | convolution fusion | flops 5445107712 | bytes 34504704 | tf_op jit(solution)/shard_map/dot_general | solution.py:31
  145.6 0.0 all-reduce.2.cloned.1.call-update
  145.6 0.0 all-gather.5.cloned.1.call-start
  145.6 0.0 copy-done
  145.6 0.3 all_to_all.14
  146.0 11.4 %all_to_all.19 = bf16[16,16,288]{2,0,1:T(8,128)(2,1)S(1)} all-to-all(bf16[16,16,288]{2,0,1:T(8,128)(2,1)S(1)} %copy.7), channel_id=1, replica_groups=mesh['row'=8,'col'=16] {'col'}, dimensions={1} | all-to-all | bytes 294912 | tf_op jit(solution)/shard_map/all_to_all | solution.py:32
  157.4 0.8 copy.8
  158.2 0.0 all-gather.5.cloned.1.call-update
  158.3 69.2 %all-reduce.2.cloned.1.call-done = f32[2048,288]{0,1:T(8,128)} async-done(((f32[2048,288]{0,1:T(8,128)}), f32[2048,288]{0,1:T(8,128)}) %all-reduce.2.cloned.1.call-update) | async-done | bytes 2359312 | tf_op jit(solution)/shard_map/psum | solution.py:33
  227.4 1.6 dynamic-slice_convert_fusion
  229.1 38.2 %all-gather.5.cloned.1.call-done = bf16[2048,288]{0,1:T(8,128)(2,1)} async-done(((bf16[256,288]{0,1:T(8,128)(2,1)}), bf16[2048,288]{0,1:T(8,128)(2,1)}) %all-gather.5.cloned.1.call-update) | async-done | bytes 1179664 | tf_op jit(solution)/shard_map/all_gather | solution.py:34
  267.3 13.0 %fusion.1 = bf16[4608,288]{0,1:T(8,128)(2,1)} fusion(bf16[2048,4608]{1,0:T(8,128)(2,1)} %all-gather.3.cloned.1.call-done, f32[4608,288]{0,1:T(8,128)} %mul.55, bf16[4608,288]{0,1:T(8,128)(2,1)S(1)} %copy-done.1, f32[2048,288]{0,1:T(8,128)} %all-reduce.2.cloned.1.call-done, bf16[2048,288]{0,1:T(8,128)(2,1)} %all-gather.5.cloned.1.call-done), kind=kOutput, calls=%fused_computation.2 | convolution fusion | flops 5448794112 | bytes 33030144 | tf_op jit(solution)/shard_map/dot_general | solution.py:41
  (3 shorter events, 0.1 us)
Async XLA Ops:
  7.2 124.8 %all-gather.3.cloned.1.call-start = ((), (), s32[]{:S(2)}) async-start(), calls=%async_computation.1 | async-start | bytes 20054016 | tf_op jit(solution)/shard_map/all_gather | solution.py:30
  7.9 219.6 %all-reduce.2.cloned.1.call-start = ((), (), s32[]{:S(2)}) async-start(), calls=%async_computation.2 | async-start | bytes 4718592 | tf_op jit(solution)/shard_map/psum | solution.py:33
  25.3 106.6 %copy-start.1 = (bf16[4608,288]{0,1:T(8,128)(2,1)S(1)}, bf16[4608,288]{0,1:T(8,128)(2,1)}, u32[]{:S(2)}) copy-start(bf16[4608,288]{0,1:T(8,128)(2,1)} %param.5) | copy-start | bytes 7962628
  33.8 111.8 %copy-start = (bf16[16,4608]{1,0:T(8,128)(2,1)S(1)}, bf16[16,4608]{1,0:T(8,128)(2,1)}, u32[]{:S(2)}) copy-start(bf16[16,4608]{1,0:T(8,128)(2,1)} %param.7) | copy-start | bytes 442372
  145.6 121.7 %all-gather.5.cloned.1.call-start = ((), (), s32[]{:S(2)}) async-start(), calls=%async_computation.3 | async-start | bytes 1327104 | tf_op jit(solution)/shard_map/all_gather | solution.py:34
Sparse Core Ops, SparseCore 0:
  10.5 121.4 all-gather.2
  145.7 81.6 all-reduce.1
  229.0 38.2 all-gather.4
where the time goes:
time: 288 us; the launch traced here: 287 us
  waiting for transfers between devices  206 us (72%)
  local copies, waits for them, and re-layouts  27.9 us (10%)
  matrix products  26.6 us (9%)
  between operations  13.8 us (5%)
  blocking collectives  11.4 us (4%)
    all_gather x1, waiting for transfers between devices, local(): gathered = lax.all_gather(hidden, 'col', axis=0, tiled=True)  98.2 us
    psum x1, waiting for transfers between devices, local(): student_all = lax.psum(partial_out, 'row')  69.2 us
    all_gather x1, waiting for transfers between devices, local(): target = lax.all_gather(columns, 'row', axis=0, tiled=True)  38.2 us
    dot_general x1, matrix products, local(): jnp.dot(gathered, quantized, preferred_element_type=jnp.float32)  13.6 us
    dot_general x1, matrix products, local(): lax.dot_general(gathered, grad_out, (((0,), (0,)), ((), ())), preferred_e...  13 us
    mul x2, local copies, waits for them, and re-layouts, quantize(): jnp.clip(levels, -127.0, 127.0) * step_cols[:, None, :]  12.6 us
    mul x2, local copies, waits for them, and re-layouts, quantize(): levels = jnp.floor(grouped * inverse_cols[:, None, :] + 0.5)  12.5 us
    all_to_all x1, blocking collectives, local(): lax.all_to_all(teacher, 'col', split_axis=1, concat_axis=0, tiled=True)  11.4 us
  transfers between devices with their start and end apart: 3, of which 3 were waited for; matrix products, arithmetic and copies ran while one was open for 10% of the time, Pallas kernels for 0%

commit v1 on v0

v1 whole, which is shorter than its diff:
```python
import functools
import math

import jax
import jax.numpy as jnp
from jax import lax
from jax.experimental import pallas as pl
from jax.experimental.pallas import tpu as pltpu
from jax.sharding import PartitionSpec as P

MESH = pl.DeviceIdType.MESH
BF16, F32 = jnp.bfloat16, jnp.float32
TILE = 96
CHUNK = 32
PIECE = 16

OWN, DOWN, UP, FAR = (0, 0), (-1, 0), (1, 0), (2, 0)
SIDE, SIDE_DOWN, SIDE_UP, SIDE_FAR = (0, 1), (-1, 1), (1, 1), (2, 1)
GROUPS = (
    ((*OWN, 0), (*OWN, 1)),
    ((*OWN, 2), (*OWN, 3)),
    ((*DOWN, 0), (*UP, 0)),
    ((*DOWN, 1), (*UP, 1)),
    ((*SIDE, 0), (*SIDE, 1)),
    ((*DOWN, 2), (*UP, 2)),
    ((*DOWN, 3), (*UP, 3)),
    ((*SIDE, 2), (*SIDE, 3)),
    ((*FAR, 0), (*FAR, 2)),
    ((*FAR, 1), (*FAR, 3)),
    ((*SIDE_DOWN, 0), (*SIDE_UP, 0)),
    ((*SIDE_DOWN, 1), (*SIDE_UP, 1)),
    ((*SIDE_FAR, 0), (*SIDE_FAR, 2)),
    ((*SIDE_DOWN, 2), (*SIDE_UP, 2)),
    ((*SIDE_FAR, 1), (*SIDE_FAR, 3)),
    ((*SIDE_DOWN, 3), (*SIDE_UP, 3)),
)
PLACE = {chunk: 4 * g + 2 * j for g, pair in enumerate(GROUPS) for j, chunk in enumerate(pair)}
STEPS = ((0, 2), (2, 3), (5, 3), (8, 2), (10, 3), (13, 2), (15, 1))
SEND_UP = (
    [((*OWN, c), (*DOWN, c)) for c in range(4)]
    + [((*DOWN, c), (*FAR, c)) for c in (0, 1)]
    + [((*SIDE, c), (*SIDE_DOWN, c)) for c in range(4)]
)
SEND_DOWN = (
    [((*OWN, c), (*UP, c)) for c in range(4)]
    + [((*UP, c), (*FAR, c)) for c in (2, 3)]
    + [((*SIDE, c), (*SIDE_UP, c)) for c in range(4)]
)
SEND_SIDE = [((*OWN, c), (*SIDE, c)) for c in range(4)] + [
    ((*FAR, c), (*SIDE_FAR, c)) for c in (0, 2, 1, 3)
]
START_UP = (0, 0, 1, 2, 3, 4, 5, 6, 7, 8)
START_DOWN = (0, 0, 1, 2, 3, 4, 5, 6, 7, 8)
START_SIDE = (0, 0, 1, 2, 5, 5, 6, 6)
ARRIVE_SIDE = (1, 2, 3, 4, 7, 8, 9, 9)
ARRIVALS = (
    [(*OWN, c) for c in range(4)]
    + [there for _, there in SEND_UP]
    + [there for _, there in SEND_DOWN]
    + [there for _, there in SEND_SIDE]
)
NUMBER = {chunk: i for i, chunk in enumerate(ARRIVALS)}
PLAN = (
    ("q", "a0"),
    ("b0",),
    ("a1", "c0"),
    ("d0", "b1"),
    ("a2", "e0", "c1"),
    ("b2", "d1"),
    ("a3", "e1", "c2"),
    ("b3", "d2"),
    ("a4", "e2", "c3"),
    ("a5", "b4", "d3", "e3", "c4", "b5"),
    ("a6", "d4", "c5", "b6", "e4", "c6", "d5", "d6", "e5", "e6"),
)


def kernel(
    factor,
    hidden, weight, scale, teacher,
    student_out, grad,
    held, keep, quant, total, parts, got_y, swap, got_x, grads, pieces, placed, cols, targets,
    up_s, up_r, down_s, down_r, side_s, side_r, core_s, core_r, load_s,
    part_s, part_r, swap_s, swap_r, gy_s, gy_r, gx_s, gx_r, fy_s, fy_r, out_s, out_r,
    col_s, col_r, row_s, row_r,
):
    row, col = lax.axis_index("row"), lax.axis_index("col")
    x_lo, y = row // 4, row % 4
    z, x_hi, core = col // 4, (col // 2) % 2, col % 2
    width = parts.shape[-1]
    depth = held.shape[-1]

    def in_col(dz, p, dc):
        return (row, ((z + dz + 4) % 4) * 4 + ((x_hi + p) % 2) * 2 + (core + dc) % 2)

    def in_row(dx, dy):
        return (((x_lo + dx) % 2) * 4 + (y + dy) % 4, col)

    def remote(src, dst, send, recv, device):
        return pltpu.make_async_remote_copy(
            src_ref=src, dst_ref=dst, send_sem=send, recv_sem=recv, device_id=device, device_id_type=MESH
        )

    up, down, side, sibling = in_col(1, 0, 0), in_col(-1, 0, 0), in_col(0, 1, 0), in_col(0, 0, 1)
    partner = in_row(1, 0)

    barrier = pltpu.get_barrier_semaphore()
    for k in range(1, 16):
        pl.semaphore_signal(barrier, inc=1, device_id=(row, (col + k) % 16), device_id_type=MESH)
    for k in range(1, 8):
        pl.semaphore_signal(barrier, inc=1, device_id=in_row(k // 4, k % 4), device_id_type=MESH)

    own = []
    for c in range(4):
        own.append(
            pltpu.make_async_copy(
                hidden.at[c], held.at[PLACE[(*OWN, c)] + core], load_s.at[c]
            )
        )
        own[c].start()
    load_weight = pltpu.make_async_copy(weight, keep, load_s.at[4])
    load_weight.start()
    pl.semaphore_wait(barrier, 22)

    sends = []

    def chunk_at(chunk):
        if chunk[:2] == OWN:
            return hidden.at[chunk[2]]
        return held.at[PLACE[chunk] + core]

    def stream(plan, send, recv, device):
        return [
            remote(chunk_at(here), held.at[PLACE[there] + core], send.at[i], recv.at[i], device)
            for i, (here, there) in enumerate(plan)
        ]

    ups = stream(SEND_UP, up_s, up_r, up)
    downs = stream(SEND_DOWN, down_s, down_r, down)
    sides = stream(SEND_SIDE, side_s, side_r, side)
    across = [
        remote(
            chunk_at(chunk), held.at[PLACE[chunk] + core], core_s.at[i], core_r.at[i], sibling
        )
        for i, chunk in enumerate(ARRIVALS)
    ]

    def start(copy):
        copy.start()
        sends.append(copy)

    def start_tick(tick):
        for copies, ticks in ((ups, START_UP), (downs, START_DOWN), (sides, START_SIDE)):
            for copy, at in zip(copies, ticks):
                if at == tick:
                    start(copy)

    t_core, t_chunk, t_half = col // 8, (col % 8) // 2, col % 2
    t_place = (2 * t_core + t_half) * 4 + t_chunk
    t_cols = [
        remote(
            teacher.at[(col + k) % 16],
            cols.at[t_place],
            col_s.at[k - 1],
            col_r.at[k - 1],
            (row, (col + k) % 16),
        )
        for k in range(1, 16)
    ]
    t_own = pltpu.make_async_copy(teacher.at[col], cols.at[t_place], load_s.at[5])
    t_rows = [
        remote(
            cols.at[pl.ds(((y + k % 4) % 4) * 4, 4)],
            targets.at[row],
            row_s.at[k - 1],
            row_r.at[k - 1],
            in_row(k // 4, k % 4),
        )
        for k in range(1, 8)
    ]

    def quantize():
        load_weight.wait()
        lane = lax.broadcasted_iota(jnp.int32, (8, width), 1)

        @pl.loop(0, depth // TILE)
        def _(i):
            e = jnp.where(lane < TILE, scale[i, 0], jnp.where(lane < 2 * TILE, scale[i, 1], scale[i, 2]))
            step = (jnp.left_shift(jnp.int32(1), e + 14).astype(F32) * 2.0 ** (-14))[0:1]
            inverse = (jnp.left_shift(jnp.int32(1), -8 - e).astype(F32) * 256.0)[0:1]
            rows = pl.ds(pl.multiple_of(i * TILE, TILE), TILE)
            levels = jnp.floor(keep[rows].astype(F32) * inverse + 0.5)
            quant[rows] = (jnp.clip(levels, -127.0, 127.0) * step).astype(BF16)
            keep[rows] = (jnp.abs(levels) <= 127.0).astype(F32).astype(BF16)

    def chunks_of(step):
        first, count = STEPS[step]
        return [chunk for g in range(first, first + count) for chunk in GROUPS[g]]

    def part_copies(s):
        first, count = STEPS[s]
        return [
            remote(
                parts.at[(y + k) % 4, :, pl.ds(first, count)],
                got_y.at[k - 1, :, pl.ds(first, count)],
                part_s.at[s, k - 1],
                part_r.at[s, k - 1],
                in_row(0, k),
            )
            for k in range(1, 4)
        ]

    def swap_copy(s):
        groups = pl.ds(*STEPS[s])
        return remote(swap.at[groups], got_x.at[groups], swap_s.at[s], swap_r.at[s], partner)

    def grad_copies(s):
        mine = grads.at[y, x_lo, pl.ds(*STEPS[s])]
        return [
            remote(mine, mine, gy_s.at[s, k - 1], gy_r.at[s, k - 1], in_row(0, k))
            for k in range(1, 4)
        ] + [remote(mine, mine, gx_s.at[s], gx_r.at[s], partner)]

    def forward_copies(s):
        theirs = grads.at[y, 1 - x_lo, pl.ds(*STEPS[s])]
        return [
            remote(theirs, theirs, fy_s.at[s, k - 1], fy_r.at[s, k - 1], in_row(0, k))
            for k in range(1, 4)
        ]

    def stage_a(s):
        for chunk in chunks_of(s):
            across[NUMBER[chunk]].wait_recv()
        first, count = STEPS[s]

        @pl.loop(first, first + count)
        def _(g):
            tokens = held[pl.ds(g * 4, 4)].reshape(4 * CHUNK, depth)
            part = jnp.dot(tokens, quant[...], preferred_element_type=F32).astype(BF16)
            for m in range(8):
                parts[m % 4, m // 4, g] = part[m * PIECE : (m + 1) * PIECE]

        for copy in part_copies(s):
            start(copy)

    def over_y(x, g):
        value = parts[y, x, g].astype(F32)
        for k in range(3):
            value = value + got_y[k, x, g].astype(F32)
        return value

    def stage_b(s):
        for copy in part_copies(s):
            copy.wait_recv()
        first, count = STEPS[s]
        for g in range(first, first + count):
            swap[g] = over_y(1 - x_lo, g).astype(BF16)
        start(swap_copy(s))

    def where_from(g):
        (dz0, p0, c0), (dz1, p1, c1) = GROUPS[g]
        t0 = ((z + dz0 + 4) % 4) * 2 + (x_hi + p0) % 2
        t1 = ((z + dz1 + 4) % 4) * 2 + (x_hi + p1) % 2
        return t0 + x_lo * (t1 - t0), c0 + x_lo * (c1 - c0)

    def piece_copy(g):
        t, c = where_from(g)
        spot = (y // 2) * 8 + 2 * c + y % 2
        return t, (
            pltpu.make_async_copy(pieces.at[g], placed.at[spot], out_r.at[spot]),
            remote(pieces.at[g], placed.at[spot], out_s.at[g], out_r.at[spot], (t, col)),
        )

    def stage_c(s):
        swap_copy(s).wait_recv()
        first, count = STEPS[s]
        for g in range(first, first + count):
            t, c = where_from(g)
            student = over_y(x_lo, g) + got_x[g].astype(F32)
            pieces[g] = student.astype(BF16)
            grads[y, x_lo, g] = ((student - targets[t, c].astype(F32)) * factor).astype(BF16)
        for copy in grad_copies(s):
            start(copy)
        for g in range(first, first + count):
            t, (here, there) = piece_copy(g)

            @pl.when(t == row)
            def _():
                here.start()

            @pl.when(t != row)
            def _():
                there.start()

    def stage_d(s):
        grad_copies(s)[3].wait_recv()
        for copy in forward_copies(s):
            start(copy)

    def stage_e(s):
        for copy in grad_copies(s)[:3] + forward_copies(s):
            copy.wait_recv()
        first, count = STEPS[s]
        g_t = jnp.concatenate(
            [grads[m % 4, m // 4, g] for g in range(first, first + count) for m in range(8)], axis=0
        ).T

        @pl.loop(0, depth // 512)
        def _(i):
            ff = pl.ds(pl.multiple_of(i * 512, 512), 512)
            tokens = held[pl.ds(4 * first, 4 * count), :, ff].reshape(4 * CHUNK * count, 512)
            part = jnp.dot(g_t, tokens, preferred_element_type=F32)
            if s == 0:
                total[:, ff] = part
            else:
                total[:, ff] += part

    stages = {"a": stage_a, "b": stage_b, "c": stage_c, "d": stage_d, "e": stage_e}

    start_tick(0)
    for copy in t_cols:
        start(copy)
    t_own.start()
    for c in range(4):
        start(across[c])

    for tick in range(11):
        if tick:
            arrived = [ups[tick - 1], downs[tick - 1]]
            names = [SEND_UP[tick - 1][1], SEND_DOWN[tick - 1][1]]
            for i, at in enumerate(ARRIVE_SIDE):
                if at == tick:
                    arrived.append(sides[i])
                    names.append(SEND_SIDE[i][1])
            for copy in arrived:
                copy.wait_recv()
            start_tick(tick)
            for name in names:
                start(across[NUMBER[name]])
        if tick == 1:
            t_own.wait()
            for copy in t_cols:
                copy.wait_recv()
            for copy in t_rows:
                start(copy)
            targets[row] = cols[pl.ds(y * 4, 4)]
        if tick == 2:
            for copy in t_rows:
                copy.wait_recv()
        for what in PLAN[tick]:
            if what == "q":
                quantize()
                for copy in own:
                    copy.wait()
            else:
                stages[what[0]](int(what[1]))

    out = quant
    writes = []
    span = 512
    for i in range(depth // span):
        ff = slice(i * span, (i + 1) * span)
        out[ff] = (total[:, ff].T * keep[ff].astype(F32)).astype(BF16)
        writes.append(pltpu.make_async_copy(out.at[pl.ds(i * span, span)], grad.at[pl.ds(i * span, span)], load_s.at[6 + i]))
        writes[-1].start()
    for spot in range(16):
        pltpu.make_async_copy(pieces.at[0], placed.at[spot], out_r.at[spot]).wait()
    write = pltpu.make_async_copy(placed, student_out, load_s.at[5])
    write.start()
    for g in range(16):
        t, (here, there) = piece_copy(g)

        @pl.when(t != row)
        def _():
            there.wait_send()

    for copy in sends:
        copy.wait_send()
    write.wait()
    for copy in writes:
        copy.wait()


def local(hidden, weight, scale_exp, teacher):
    block, depth = hidden.shape
    width = weight.shape[1]
    tokens = block * lax.axis_size("col")
    groups, steps = len(GROUPS), len(STEPS)
    hidden = hidden.reshape(block // CHUNK, CHUNK, depth)
    teacher = teacher.reshape(PIECE, -1, width).transpose(1, 0, 2)
    dma = pltpu.SemaphoreType.DMA
    anywhere = pl.BlockSpec(memory_space=pl.ANY)
    student_out, grad = pl.pallas_call(
        functools.partial(kernel, 1.0 / math.sqrt(tokens)),
        out_shape=(
            jax.ShapeDtypeStruct((16, PIECE, width), BF16),
            jax.ShapeDtypeStruct((depth, width), BF16),
        ),
        in_specs=[anywhere, anywhere, pl.BlockSpec(memory_space=pltpu.SMEM), anywhere],
        out_specs=(anywhere, anywhere),
        scratch_shapes=[
            pltpu.VMEM((4 * groups, CHUNK, depth), BF16),
            pltpu.VMEM((depth, width), BF16),
            pltpu.VMEM((depth, width), BF16),
            pltpu.VMEM((width, depth), F32),
            pltpu.VMEM((4, 2, groups, PIECE, width), BF16),
            pltpu.VMEM((3, 2, groups, PIECE, width), BF16),
            pltpu.VMEM((groups, PIECE, width), BF16),
            pltpu.VMEM((groups, PIECE, width), BF16),
            pltpu.VMEM((4, 2, groups, PIECE, width), BF16),
            pltpu.VMEM((groups, PIECE, width), BF16),
            pltpu.VMEM((16, PIECE, width), BF16),
            pltpu.VMEM((16, PIECE, width), BF16),
            pltpu.VMEM((8, 4, PIECE, width), BF16),
            dma((10,)), dma((10,)), dma((10,)), dma((10,)), dma((8,)), dma((8,)),
            dma((32,)), dma((32,)), dma((16,)),
            dma((steps, 3)), dma((steps, 3)), dma((steps,)), dma((steps,)),
            dma((steps, 3)), dma((steps, 3)), dma((steps,)), dma((steps,)),
            dma((steps, 3)), dma((steps, 3)), dma((groups,)), dma((16,)),
            dma((15,)), dma((15,)), dma((7,)), dma((7,)),
        ],
        compiler_params=pltpu.CompilerParams(
            collective_id=0, has_side_effects=True, vmem_limit_bytes=56 * 2**20
        ),
        cost_estimate=pl.CostEstimate(
            flops=4 * tokens * depth * width, bytes_accessed=3 * depth * width, transcendentals=0
        ),
    )(hidden, weight, scale_exp, teacher)
    return (student_out.reshape(16 * PIECE, width), grad)


def solution(mesh):
    placed = (P("col", "row"), P("row", "col"), P("row", "col"), P(("row", "col"), None))
    return jax.shard_map(
        local,
        mesh=mesh,
        in_specs=placed,
        out_specs=(P("row", "col"), P("row", "col")),
        check_vma=False,
    )
```

time: 288 us -> 142 us (0.49)
  waiting for transfers between devices: 206 us -> 0 us
  Pallas kernels: 0 us -> 127 us
  matrix products: 26.6 us -> 0 us
  local copies, waits for them, and re-layouts: 27.9 us -> 14.3 us
  between operations: 13.8 us -> 0.64 us
  blocking collectives: 11.4 us -> 0 us
    all_gather x2 -> x0, waiting for transfers between devices: 136 us -> none  [the longest x1 98.2 us: local(): gathered = lax.all_gather(hidden, 'col', axis=0, tiled=True)]
    pallas_call x0 -> x1, Pallas kernels: none -> 127 us  [local(): pl.pallas_call(functools.partial(kernel, 1.0 / math.sqrt(tokens)), out_sh...]
    psum x1 -> x0, waiting for transfers between devices: 69.2 us -> none  [local(): student_all = lax.psum(partial_out, 'row')]
    dot_general x2 -> x0, matrix products: 26.6 us -> none  [the longest x1 13.6 us: local(): jnp.dot(gathered, quantized, preferred_element_type=jnp.float32)]
    mul x4 -> x0, local copies, waits for them, and re-layouts: 25.1 us -> none  [the longest x2 12.6 us: quantize(): jnp.clip(levels, -127.0, 127.0) * step_cols[:, None, :]]
    unnamed x4, local copies, waits for them, and re-layouts: 0.01 us -> 12.4 us
    all_to_all x1 -> x0, blocking collectives: 11.4 us -> none  [local(): lax.all_to_all(teacher, 'col', split_axis=1, concat_axis=0, tiled=True)]
  transfers between devices with their start and end apart: 3 -> 0, of which waited for: 3 -> 0; matrix products, arithmetic and copies ran while one was open for 10% -> 0% of each run, Pallas kernels for 0% -> 0%
where the time goes in v1:
time: 142 us
  Pallas kernels  127 us (89%)
  local copies, waits for them, and re-layouts  14.3 us (10%)
    pallas_call x1, Pallas kernels, local(): pl.pallas_call(functools.partial(kernel, 1.0 / math.sqrt(tokens)), out_sh...  127 us
    unnamed x4, local copies, waits for them, and re-layouts  12.4 us

profile of v1, /device:TPU:0, one launch (start us, length us, event | category | flops | bytes accessed | tf_op | source)
XLA Modules:
  0.0 142.0 jit_solution(908529688826268041)
XLA Ops:
  0.6 1.4 copy.12.scale
  2.0 1.2 reshape.14
  3.2 0.7 copy.16
  3.9 4.7 %copy.11.weight = bf16[4608,288]{1,0:T(8,128)(2,1)} copy(bf16[4608,288]{0,1:T(8,128)(2,1)} %param.5) | data formatting | bytes 5308416 | tf_op args[1]
  8.6 127.0 %shard_map.59 = (bf16[16,16,288]{2,1,0:T(8,128)(2,1)}, bf16[4608,288]{1,0:T(8,128)(2,1)}) custom-call(bf16[4,32,4608]{2,1,0:T(8,128)(2,1)} %bitcast.7, bf16[4608,288]{1,0:T(8,128)(2,1)} %copy.11.weight, s32[48,3]{1,0:T(8,128)} %copy.12.scale, bf16[16,16,288]{2,1,0:T(8,128)(2,1)} %bitcast.5), custom_call_target="tpu_custom_call" | custom-call | flops 10871635968 | bytes 3981312 | tf_op jit(solution)/shard_map/pallas_call | solution.py:393
  135.7 1.7 %copy.13 = bf16[256,288]{0,1:T(8,128)(2,1)} copy(bf16[256,288]{1,0:T(8,128)(2,1)} %bitcast.6) | data formatting | bytes 294912
  137.4 4.6 %copy.14 = bf16[4608,288]{0,1:T(8,128)(2,1)} copy(bf16[4608,288]{1,0:T(8,128)(2,1)} %get-tuple-element.9) | data formatting | bytes 5308416

commit v2 on v1

--- a/solution.py
+++ b/solution.py
@@ -22,20 +22,20 @@
     ((*DOWN, 0), (*UP, 0)),
     ((*DOWN, 1), (*UP, 1)),
     ((*SIDE, 0), (*SIDE, 1)),
+    ((*SIDE, 2), (*SIDE, 3)),
     ((*DOWN, 2), (*UP, 2)),
     ((*DOWN, 3), (*UP, 3)),
-    ((*SIDE, 2), (*SIDE, 3)),
     ((*FAR, 0), (*FAR, 2)),
     ((*FAR, 1), (*FAR, 3)),
     ((*SIDE_DOWN, 0), (*SIDE_UP, 0)),
     ((*SIDE_DOWN, 1), (*SIDE_UP, 1)),
     ((*SIDE_FAR, 0), (*SIDE_FAR, 2)),
+    ((*SIDE_FAR, 1), (*SIDE_FAR, 3)),
     ((*SIDE_DOWN, 2), (*SIDE_UP, 2)),
-    ((*SIDE_FAR, 1), (*SIDE_FAR, 3)),
     ((*SIDE_DOWN, 3), (*SIDE_UP, 3)),
 )
 PLACE = {chunk: 4 * g + 2 * j for g, pair in enumerate(GROUPS) for j, chunk in enumerate(pair)}
-STEPS = ((0, 2), (2, 3), (5, 3), (8, 2), (10, 3), (13, 2), (15, 1))
+STEPS = ((0, 2), (2, 2), (4, 2), (6, 2), (8, 2), (10, 2), (12, 2), (14, 1), (15, 1))
 SEND_UP = (
     [((*OWN, c), (*DOWN, c)) for c in range(4)]
     + [((*DOWN, c), (*FAR, c)) for c in (0, 1)]
@@ -61,17 +61,17 @@
 )
 NUMBER = {chunk: i for i, chunk in enumerate(ARRIVALS)}
 PLAN = (
-    ("q", "a0"),
-    ("b0",),
-    ("a1", "c0"),
-    ("d0", "b1"),
-    ("a2", "e0", "c1"),
-    ("b2", "d1"),
-    ("a3", "e1", "c2"),
-    ("b3", "d2"),
-    ("a4", "e2", "c3"),
-    ("a5", "b4", "d3", "e3", "c4", "b5"),
-    ("a6", "d4", "c5", "b6", "e4", "c6", "d5", "d6", "e5", "e6"),
+    "t q a0",
+    "b0",
+    "a1",
+    "c0 b1",
+    "a2 a3",
+    "d0 c1 b2 b3",
+    "a4 e0",
+    "d1 c2 c3 b4",
+    "a5 e1",
+    "a6 a7 d2 d3 c4 b5",
+    "a8 b6 b7 c5 d4 e2 b8 c6 c7 d5 e3 c8 d6 d7 e4 e5 d8 e6 f",
 )
 
 
@@ -79,7 +79,7 @@
     factor,
     hidden, weight, scale, teacher,
     student_out, grad,
-    held, keep, quant, total, parts, got_y, swap, got_x, grads, pieces, placed, cols, targets,
+    held, keep, quant, total, whole, spread, parts, got_y, swap, got_x, grads, pieces, placed, turned, cols, targets,
     up_s, up_r, down_s, down_r, side_s, side_r, core_s, core_r, load_s,
     part_s, part_r, swap_s, swap_r, gy_s, gy_r, gx_s, gx_r, fy_s, fy_r, out_s, out_r,
     col_s, col_r, row_s, row_r,
@@ -89,6 +89,7 @@
     z, x_hi, core = col // 4, (col // 2) % 2, col % 2
     width = parts.shape[-1]
     depth = held.shape[-1]
+    steps = len(STEPS)
 
     def in_col(dz, p, dc):
         return (row, ((z + dz + 4) % 4) * 4 + ((x_hi + p) % 2) * 2 + (core + dc) % 2)
@@ -120,6 +121,8 @@
         own[c].start()
     load_weight = pltpu.make_async_copy(weight, keep, load_s.at[4])
     load_weight.start()
+    load_teacher = pltpu.make_async_copy(teacher, whole, load_s.at[6])
+    load_teacher.start()
     pl.semaphore_wait(barrier, 22)
 
     sends = []
@@ -159,7 +162,7 @@
     t_place = (2 * t_core + t_half) * 4 + t_chunk
     t_cols = [
         remote(
-            teacher.at[(col + k) % 16],
+            spread.at[(col + k) % 16],
             cols.at[t_place],
             col_s.at[k - 1],
             col_r.at[k - 1],
@@ -167,7 +170,7 @@
         )
         for k in range(1, 16)
     ]
-    t_own = pltpu.make_async_copy(teacher.at[col], cols.at[t_place], load_s.at[5])
+    t_own = pltpu.make_async_copy(spread.at[col], cols.at[t_place], load_s.at[5])
     t_rows = [
         remote(
             cols.at[pl.ds(((y + k % 4) % 4) * 4, 4)],
@@ -179,19 +182,32 @@
         for k in range(1, 8)
     ]
 
+    def spread_teacher():
+        load_teacher.wait()
+        for i in range(16):
+            spread[i] = whole[:, i * width : (i + 1) * width]
+        for copy in t_cols:
+            start(copy)
+        t_own.start()
+
     def quantize():
         load_weight.wait()
-        lane = lax.broadcasted_iota(jnp.int32, (8, width), 1)
-
-        @pl.loop(0, depth // TILE)
+        span = 4 * TILE
+        lane = lax.broadcasted_iota(jnp.int32, (8, span), 1)
+
+        @pl.loop(0, depth // span)
         def _(i):
-            e = jnp.where(lane < TILE, scale[i, 0], jnp.where(lane < 2 * TILE, scale[i, 1], scale[i, 2]))
-            step = (jnp.left_shift(jnp.int32(1), e + 14).astype(F32) * 2.0 ** (-14))[0:1]
-            inverse = (jnp.left_shift(jnp.int32(1), -8 - e).astype(F32) * 256.0)[0:1]
-            rows = pl.ds(pl.multiple_of(i * TILE, TILE), TILE)
-            levels = jnp.floor(keep[rows].astype(F32) * inverse + 0.5)
-            quant[rows] = (jnp.clip(levels, -127.0, 127.0) * step).astype(BF16)
-            keep[rows] = (jnp.abs(levels) <= 127.0).astype(F32).astype(BF16)
+            ff = pl.ds(pl.multiple_of(i * span, span), span)
+            for j in range(width // TILE):
+                e = jnp.full((8, span), scale[j, 4 * i], jnp.int32)
+                for k in range(1, 4):
+                    e = jnp.where(lane < k * TILE, e, scale[j, 4 * i + k])
+                step = (jnp.left_shift(jnp.int32(1), e + 14).astype(F32) * 2.0 ** (-14))[0:1]
+                inverse = (jnp.left_shift(jnp.int32(1), -8 - e).astype(F32) * 256.0)[0:1]
+                rows = slice(j * TILE, (j + 1) * TILE)
+                levels = jnp.floor(keep[rows, ff].astype(F32) * inverse + 0.5)
+                quant[rows, ff] = (jnp.clip(levels, -127.0, 127.0) * step).astype(BF16)
+                keep[rows, ff] = (jnp.abs(levels) <= 127.0).astype(F32).astype(BF16)
 
     def chunks_of(step):
         first, count = STEPS[step]
@@ -228,17 +244,22 @@
             for k in range(1, 4)
         ]
 
+    def tokens_of(first, count, ff):
+        return held[4 * first : 4 * (first + count), :, ff].reshape(4 * CHUNK * count, -1)
+
     def stage_a(s):
         for chunk in chunks_of(s):
             across[NUMBER[chunk]].wait_recv()
         first, count = STEPS[s]
 
-        @pl.loop(first, first + count)
-        def _(g):
-            tokens = held[pl.ds(g * 4, 4)].reshape(4 * CHUNK, depth)
-            part = jnp.dot(tokens, quant[...], preferred_element_type=F32).astype(BF16)
+        part = lax.dot_general(
+            quant[...], tokens_of(first, count, slice(None)), (((1,), (1,)), ((), ())),
+            preferred_element_type=F32,
+        ).T.astype(BF16)
+        for g in range(count):
             for m in range(8):
-                parts[m % 4, m // 4, g] = part[m * PIECE : (m + 1) * PIECE]
+                at = (g * 8 + m) * PIECE
+                parts[m % 4, m // 4, first + g] = part[at : at + PIECE]
 
         for copy in part_copies(s):
             start(copy)
@@ -297,30 +318,49 @@
         for copy in forward_copies(s):
             start(copy)
 
-    def stage_e(s):
+    def gradients(first, count):
+        pieces_of = [grads[m % 4, m // 4, g] for g in range(first, first + count) for m in range(8)]
+        return jnp.concatenate(pieces_of, axis=0).T
+
+    def wait_gradients(s):
         for copy in grad_copies(s)[:3] + forward_copies(s):
             copy.wait_recv()
+
+    def stage_e(s):
+        wait_gradients(s)
         first, count = STEPS[s]
-        g_t = jnp.concatenate(
-            [grads[m % 4, m // 4, g] for g in range(first, first + count) for m in range(8)], axis=0
-        ).T
-
-        @pl.loop(0, depth // 512)
-        def _(i):
-            ff = pl.ds(pl.multiple_of(i * 512, 512), 512)
-            tokens = held[pl.ds(4 * first, 4 * count), :, ff].reshape(4 * CHUNK * count, 512)
-            part = jnp.dot(g_t, tokens, preferred_element_type=F32)
-            if s == 0:
-                total[:, ff] = part
-            else:
-                total[:, ff] += part
+        part = jnp.dot(gradients(first, count), tokens_of(first, count, slice(None)), preferred_element_type=F32)
+        if s == 0:
+            total[...] = part
+        else:
+            total[...] += part
+
+    writes = []
+
+    def finish():
+        for s in (steps - 2, steps - 1):
+            wait_gradients(s)
+        first = STEPS[steps - 2][0]
+        count = len(GROUPS) - first
+        g_t = gradients(first, count)
+        span = depth // 4
+        for i in range(4):
+            ff = slice(i * span, (i + 1) * span)
+            part = jnp.dot(g_t, tokens_of(first, count, ff), preferred_element_type=F32)
+            quant[:, ff] = ((total[:, ff] + part) * keep[:, ff].astype(F32)).astype(BF16)
+            write = pltpu.make_async_copy(quant.at[:, ff], grad.at[:, ff], load_s.at[7 + i])
+            write.start()
+            writes.append(write)
+        for spot in range(16):
+            pltpu.make_async_copy(pieces.at[0], placed.at[spot], out_r.at[spot]).wait()
+        turned[...] = placed[...].reshape(16 * PIECE, width).T
+        write = pltpu.make_async_copy(turned, student_out, load_s.at[5])
+        write.start()
+        writes.append(write)
 
     stages = {"a": stage_a, "b": stage_b, "c": stage_c, "d": stage_d, "e": stage_e}
 
     start_tick(0)
-    for copy in t_cols:
-        start(copy)
-    t_own.start()
     for c in range(4):
         start(across[c])
 
@@ -347,26 +387,18 @@
         if tick == 2:
             for copy in t_rows:
                 copy.wait_recv()
-        for what in PLAN[tick]:
-            if what == "q":
+        for what in PLAN[tick].split():
+            if what == "t":
+                spread_teacher()
+            elif what == "q":
                 quantize()
                 for copy in own:
                     copy.wait()
+            elif what == "f":
+                finish()
             else:
                 stages[what[0]](int(what[1]))
 
-    out = quant
-    writes = []
-    span = 512
-    for i in range(depth // span):
-        ff = slice(i * span, (i + 1) * span)
-        out[ff] = (total[:, ff].T * keep[ff].astype(F32)).astype(BF16)
-        writes.append(pltpu.make_async_copy(out.at[pl.ds(i * span, span)], grad.at[pl.ds(i * span, span)], load_s.at[6 + i]))
-        writes[-1].start()
-    for spot in range(16):
-        pltpu.make_async_copy(pieces.at[0], placed.at[spot], out_r.at[spot]).wait()
-    write = pltpu.make_async_copy(placed, student_out, load_s.at[5])
-    write.start()
     for g in range(16):
         t, (here, there) = piece_copy(g)
 
@@ -376,7 +408,6 @@
 
     for copy in sends:
         copy.wait_send()
-    write.wait()
     for copy in writes:
         copy.wait()
 
@@ -387,22 +418,23 @@
     tokens = block * lax.axis_size("col")
     groups, steps = len(GROUPS), len(STEPS)
     hidden = hidden.reshape(block // CHUNK, CHUNK, depth)
-    teacher = teacher.reshape(PIECE, -1, width).transpose(1, 0, 2)
     dma = pltpu.SemaphoreType.DMA
     anywhere = pl.BlockSpec(memory_space=pl.ANY)
     student_out, grad = pl.pallas_call(
         functools.partial(kernel, 1.0 / math.sqrt(tokens)),
         out_shape=(
-            jax.ShapeDtypeStruct((16, PIECE, width), BF16),
-            jax.ShapeDtypeStruct((depth, width), BF16),
+            jax.ShapeDtypeStruct((width, 16 * PIECE), BF16),
+            jax.ShapeDtypeStruct((width, depth), BF16),
         ),
         in_specs=[anywhere, anywhere, pl.BlockSpec(memory_space=pltpu.SMEM), anywhere],
         out_specs=(anywhere, anywhere),
         scratch_shapes=[
             pltpu.VMEM((4 * groups, CHUNK, depth), BF16),
-            pltpu.VMEM((depth, width), BF16),
-            pltpu.VMEM((depth, width), BF16),
+            pltpu.VMEM((width, depth), BF16),
+            pltpu.VMEM((width, depth), BF16),
             pltpu.VMEM((width, depth), F32),
+            pltpu.VMEM((16, depth), BF16),
+            pltpu.VMEM((16, PIECE, width), BF16),
             pltpu.VMEM((4, 2, groups, PIECE, width), BF16),
             pltpu.VMEM((3, 2, groups, PIECE, width), BF16),
             pltpu.VMEM((groups, PIECE, width), BF16),
@@ -410,6 +442,7 @@
             pltpu.VMEM((4, 2, groups, PIECE, width), BF16),
             pltpu.VMEM((groups, PIECE, width), BF16),
             pltpu.VMEM((16, PIECE, width), BF16),
+            pltpu.VMEM((width, 16 * PIECE), BF16),
             pltpu.VMEM((16, PIECE, width), BF16),
             pltpu.VMEM((8, 4, PIECE, width), BF16),
             dma((10,)), dma((10,)), dma((10,)), dma((10,)), dma((8,)), dma((8,)),
@@ -425,8 +458,8 @@
         cost_estimate=pl.CostEstimate(
             flops=4 * tokens * depth * width, bytes_accessed=3 * depth * width, transcendentals=0
         ),
-    )(hidden, weight, scale_exp, teacher)
-    return (student_out.reshape(16 * PIECE, width), grad)
+    )(hidden, weight.T, scale_exp.T, teacher)
+    return (student_out.T, grad.T)
 
 
 def solution(mesh):

time: 142 us -> 118 us (0.83); the launches traced: 142 us -> 116 us
  Pallas kernels: 127 us -> 111 us
  local copies, waits for them, and re-layouts: 14.3 us -> 5 us
    pallas_call x1, Pallas kernels: 127 us -> 111 us  [local(): pl.pallas_call(functools.partial(kernel, 1.0 / math.sqrt(tokens)), out_sh...]
    unnamed x4 -> x2, local copies, waits for them, and re-layouts: 12.4 us -> 5 us
    reshape x2 -> x0, local copies, waits for them, and re-layouts: 1.91 us -> none  [local(): teacher = teacher.reshape(PIECE, -1, width).transpose(1, 0, 2)]
where the time goes in v2:
time: 118 us; the launch traced here: 116 us
  Pallas kernels  111 us (94%)
  local copies, waits for them, and re-layouts  5 us (4%)
    pallas_call x1, Pallas kernels, local(): pl.pallas_call(functools.partial(kernel, 1.0 / math.sqrt(tokens)), out_sh...  111 us
    unnamed x2, local copies, waits for them, and re-layouts  5 us

profile of v2, /device:TPU:0, one launch (start us, length us, event | category | flops | bytes accessed | tf_op | source)
XLA Modules:
  0.0 116.4 jit_solution(15835336911504101678)
XLA Ops:
  0.6 110.7 %shard_map.59 = (bf16[288,256]{1,0:T(8,128)(2,1)}, bf16[288,4608]{1,0:T(8,128)(2,1)}) custom-call(bf16[4,32,4608]{2,1,0:T(8,128)(2,1)} %bitcast.8, bf16[288,4608]{1,0:T(8,128)(2,1)} %bitcast.7, s32[3,48]{1,0:T(4,128)} %bitcast.9, bf16[16,4608]{1,0:T(8,128)(2,1)} %teacher.1), custom_call_target="tpu_custom_call" | custom-call | flops 10871635968 | bytes 3981312 | tf_op jit(solution)/shard_map/pallas_call | solution.py:423
  111.4 1.6 %copy.8 = bf16[256,288]{0,1:T(8,128)(2,1)} copy(bf16[256,288]{0,1:T(8,128)(2,1)} %bitcast.6) | data formatting | bytes 294912
  113.0 3.4 %copy.9 = bf16[4608,288]{0,1:T(8,128)(2,1)} copy(bf16[4608,288]{0,1:T(8,128)(2,1)} %bitcast.5) | data formatting | bytes 5308416

commit v3 on v2

v3 whole, which is shorter than its diff:
```python
import functools
import math

import jax
import jax.numpy as jnp
from jax import lax
from jax.experimental import pallas as pl
from jax.experimental.pallas import tpu as pltpu
from jax.sharding import PartitionSpec as P

MESH = pl.DeviceIdType.MESH
BF16, F32 = jnp.bfloat16, jnp.float32
TILE = 96
CHUNK = 32
PIECE = 16

OWN, DOWN, UP, FAR = (0, 0), (-1, 0), (1, 0), (2, 0)
SIDE, SIDE_DOWN, SIDE_UP, SIDE_FAR = (0, 1), (-1, 1), (1, 1), (2, 1)
GROUPS = (
    ((*OWN, 0), (*OWN, 1)),
    ((*OWN, 2), (*OWN, 3)),
    ((*DOWN, 0), (*UP, 2)),
    ((*DOWN, 1), (*UP, 3)),
    ((*SIDE, 0), (*SIDE, 1)),
    ((*SIDE, 2), (*SIDE, 3)),
    ((*FAR, 0), (*FAR, 2)),
    ((*FAR, 1), (*FAR, 3)),
    ((*DOWN, 2), (*UP, 0)),
    ((*DOWN, 3), (*UP, 1)),
    ((*SIDE_DOWN, 0), (*SIDE_UP, 0)),
    ((*SIDE_DOWN, 1), (*SIDE_UP, 1)),
    ((*SIDE_FAR, 0), (*SIDE_FAR, 2)),
    ((*SIDE_FAR, 1), (*SIDE_FAR, 3)),
    ((*SIDE_DOWN, 2), (*SIDE_UP, 2)),
    ((*SIDE_DOWN, 3), (*SIDE_UP, 3)),
)
PLACE = {chunk: 4 * g + 2 * j for g, pair in enumerate(GROUPS) for j, chunk in enumerate(pair)}
STEPS = ((0, 2), (2, 2), (4, 2), (6, 2), (8, 2), (10, 2), (12, 2), (14, 1), (15, 1))
SEND_UP = [
    ((*OWN, 0), (*DOWN, 0)),
    ((*OWN, 1), (*DOWN, 1)),
    ((*DOWN, 0), (*FAR, 0)),
    ((*OWN, 2), (*DOWN, 2)),
    ((*DOWN, 1), (*FAR, 1)),
    ((*OWN, 3), (*DOWN, 3)),
] + [((*SIDE, c), (*SIDE_DOWN, c)) for c in range(4)]
SEND_DOWN = [
    ((*OWN, 2), (*UP, 2)),
    ((*OWN, 3), (*UP, 3)),
    ((*UP, 2), (*FAR, 2)),
    ((*OWN, 0), (*UP, 0)),
    ((*UP, 3), (*FAR, 3)),
    ((*OWN, 1), (*UP, 1)),
] + [((*SIDE, c), (*SIDE_UP, c)) for c in range(4)]
SEND_SIDE = [((*OWN, c), (*SIDE, c)) for c in range(4)] + [
    ((*FAR, c), (*SIDE_FAR, c)) for c in (0, 2, 1, 3)
]
START_UP = (0, 0, 1, 2, 3, 4, 5, 6, 7, 8)
START_DOWN = (0, 0, 1, 2, 3, 4, 5, 6, 7, 8)
START_SIDE = (0, 1, 2, 3, 4, 5, 6, 7)
ARRIVE_SIDE = (2, 3, 4, 5, 6, 7, 8, 9)
ARRIVALS = (
    [(*OWN, c) for c in range(4)]
    + [there for _, there in SEND_UP]
    + [there for _, there in SEND_DOWN]
    + [there for _, there in SEND_SIDE]
)
NUMBER = {chunk: i for i, chunk in enumerate(ARRIVALS)}
PLAN = (
    ("q", "a0",),
    ("x",),
    ("rows", "b0", "x", "a1",),
    ("x",),
    ("targets", "c0", "b1", "x",),
    ("d0", "c1", "x", "a3", "a2",),
    ("d1", "x", "a4", "e0",),
    ("b3", "b2", "x", "e1",),
    ("c3", "c2", "b4", "a5",),
    ("d3", "d2", "c4", "a7", "a6",),
    ("d4", "b5", "a8", "b7", "b6", "e23", "c5", "c7", "c6", "r", "e4", "d5", "d7", "d6", "e56", "f",),
)


def kernel(
    factor,
    hidden, weight, scale, teacher,
    student_out, grad,
    held, keep, quant, total, whole, spread, parts, got_y, swap, got_x, got_last, grads, pieces, placed, cols, targets,
    load, sent, up_r, down_r, side_r, core_r, part_r, swap_r, grad_y_r, grad_x_r, out_s, out_r, last_r, teacher_r,
):
    row, col = lax.axis_index("row"), lax.axis_index("col")
    x_lo, y = row // 4, row % 4
    z, x_hi, core = col // 4, (col // 2) % 2, col % 2
    width = parts.shape[-1]
    depth = held.shape[-1]
    steps = len(STEPS)
    last = STEPS[-1][0]

    def in_col(dz, p, dc):
        return (row, ((z + dz + 4) % 4) * 4 + ((x_hi + p) % 2) * 2 + (core + dc) % 2)

    def in_row(dx, dy):
        return (((x_lo + dx) % 2) * 4 + (y + dy) % 4, col)

    def remote(src, dst, send, recv, device):
        return pltpu.make_async_remote_copy(
            src_ref=src, dst_ref=dst, send_sem=send, recv_sem=recv, device_id=device, device_id_type=MESH
        )

    up, down, side, sibling = in_col(1, 0, 0), in_col(-1, 0, 0), in_col(0, 1, 0), in_col(0, 0, 1)
    partner = in_row(1, 0)

    barrier = pltpu.get_barrier_semaphore()
    for k in range(1, 16):
        pl.semaphore_signal(barrier, inc=1, device_id=(row, (col + k) % 16), device_id_type=MESH)
    for k in range(1, 8):
        pl.semaphore_signal(barrier, inc=1, device_id=in_row(k // 4, k % 4), device_id_type=MESH)

    own = []
    for c in range(4):
        own.append(
            pltpu.make_async_copy(
                hidden.at[c], held.at[PLACE[(*OWN, c)] + core], load.at[c]
            )
        )
        own[c].start()
    load_weight = pltpu.make_async_copy(weight, keep, load.at[4])
    load_weight.start()
    load_teacher = pltpu.make_async_copy(teacher, whole, load.at[5])
    load_teacher.start()
    pl.semaphore_wait(barrier, 22)

    def chunks_of(step):
        first, count = STEPS[step]
        return [chunk for g in range(first, first + count) for chunk in GROUPS[g]]

    def chunk_at(chunk):
        if chunk[:2] == OWN:
            return hidden.at[chunk[2]]
        return held.at[PLACE[chunk] + core]

    def stream(plan, recv, device):
        return [
            remote(chunk_at(here), held.at[PLACE[there] + core], sent.at[0], recv.at[i], device)
            for i, (here, there) in enumerate(plan)
        ]

    ups = stream(SEND_UP, up_r, up)
    downs = stream(SEND_DOWN, down_r, down)
    sides = stream(SEND_SIDE, side_r, side)
    step_of = {chunk: s for s in range(steps) for chunk in chunks_of(s)}
    across = [
        remote(
            chunk_at(chunk), held.at[PLACE[chunk] + core], sent.at[0], core_r.at[step_of[chunk]], sibling
        )
        for chunk in ARRIVALS
    ]

    def arrived_bytes(ref, sem):
        pltpu.make_async_copy(ref, ref, sem).wait()

    def start_tick(tick):
        for copies, ticks in ((ups, START_UP), (downs, START_DOWN)):
            for copy, at in zip(copies, ticks):
                if at == tick:
                    copy.start()

    def start_side(tick):
        for copy, at in zip(sides, START_SIDE):
            if at == tick:
                copy.start()

    t_core, t_chunk, t_half = col // 8, (col % 8) // 2, col % 2
    t_place = (2 * t_core + t_half) * 4 + t_chunk
    t_cols = [
        remote(
            spread.at[(col + k) % 16],
            cols.at[t_place],
            sent.at[6],
            teacher_r.at[0],
            (row, (col + k) % 16),
        )
        for k in range(1, 16)
    ]
    t_own = pltpu.make_async_copy(spread.at[col], cols.at[t_place], load.at[5])
    t_rows = [
        remote(
            cols.at[pl.ds(((y + k % 4) % 4) * 4, 4)],
            targets.at[row],
            sent.at[7],
            teacher_r.at[1],
            in_row(k // 4, k % 4),
        )
        for k in range(1, 8)
    ]

    def quantize():
        load_weight.wait()
        span = 4 * TILE
        lane = lax.broadcasted_iota(jnp.int32, (8, span), 1)

        @pl.loop(0, depth // span)
        def _(i):
            ff = pl.ds(pl.multiple_of(i * span, span), span)
            for j in range(width // TILE):
                e = jnp.full((8, span), scale[j, 4 * i], jnp.int32)
                for k in range(1, 4):
                    e = jnp.where(lane < k * TILE, e, scale[j, 4 * i + k])
                step = (jnp.left_shift(jnp.int32(1), e + 14).astype(F32) * 2.0 ** (-14))[0:1]
                inverse = (jnp.left_shift(jnp.int32(1), -8 - e).astype(F32) * 256.0)[0:1]
                rows = slice(j * TILE, (j + 1) * TILE)
                levels = jnp.floor(keep[rows, ff].astype(F32) * inverse + 0.5)
                quant[rows, ff] = (jnp.clip(levels, -127.0, 127.0) * step).astype(BF16)
                keep[rows, ff] = (jnp.abs(levels) <= 127.0).astype(F32).astype(BF16)

    def part_copies(s):
        first, count = STEPS[s]
        return [
            remote(
                parts.at[(y + k) % 4, :, pl.ds(first, count)],
                got_y.at[k - 1, :, pl.ds(first, count)],
                sent.at[1],
                part_r.at[s],
                in_row(0, k),
            )
            for k in range(1, 4)
        ]

    def swap_copy(s):
        groups = pl.ds(*STEPS[s])
        return remote(swap.at[groups], got_x.at[groups], sent.at[2], swap_r.at[s], partner)

    def grad_copies(s):
        mine = grads.at[y, x_lo, pl.ds(*STEPS[s])]
        return [
            remote(mine, mine, sent.at[3], grad_y_r.at[s], in_row(0, k))
            for k in range(1, 4)
        ] + [remote(mine, mine, sent.at[4], grad_x_r.at[s], partner)]

    def forward_copies(s):
        theirs = grads.at[y, 1 - x_lo, pl.ds(*STEPS[s])]
        return [
            remote(theirs, theirs, sent.at[3], grad_y_r.at[s], in_row(0, k))
            for k in range(1, 4)
        ]

    def tokens_of(first, count, ff):
        return held[4 * first : 4 * (first + count), :, ff].reshape(4 * CHUNK * count, -1)

    def stage_a(s):
        first, count = STEPS[s]
        arrived_bytes(held.at[pl.ds(0, 2 * count)], core_r.at[s])

        part = lax.dot_general(
            quant[...], tokens_of(first, count, slice(None)), (((1,), (1,)), ((), ())),
            preferred_element_type=F32,
        ).T.astype(BF16)
        for g in range(count):
            for m in range(8):
                at = (g * 8 + m) * PIECE
                parts[m % 4, m // 4, first + g] = part[at : at + PIECE]

        for copy in last_parts() if s == steps - 1 else part_copies(s):
            copy.start()

    def last_parts():
        return [
            remote(
                parts.at[(y + k % 4) % 4, (x_lo + k // 4) % 2, last],
                got_last.at[k - 1],
                sent.at[5],
                last_r.at[0],
                in_row(k // 4, k % 4),
            )
            for k in range(1, 8)
        ]

    def last_grads():
        mine = grads.at[y, x_lo, last]
        return [
            remote(mine, mine, sent.at[5], last_r.at[1], in_row(k // 4, k % 4))
            for k in range(1, 8)
        ]

    def last_sum():
        arrived_bytes(got_last, last_r.at[0])
        student = parts[y, x_lo, last].astype(F32)
        for k in range(7):
            student = student + got_last[k].astype(F32)
        give(last, student)
        for copy in last_grads():
            copy.start()
        place(last)

    def over_y(x, g):
        value = parts[y, x, g].astype(F32)
        for k in range(3):
            value = value + got_y[k, x, g].astype(F32)
        return value

    def stage_b(s):
        first, count = STEPS[s]
        arrived_bytes(got_y.at[:, :, pl.ds(first, count)], part_r.at[s])
        for g in range(first, first + count):
            swap[g] = over_y(1 - x_lo, g).astype(BF16)
        swap_copy(s).start()

    def where_from(g):
        (dz0, p0, c0), (dz1, p1, c1) = GROUPS[g]
        t0 = ((z + dz0 + 4) % 4) * 2 + (x_hi + p0) % 2
        t1 = ((z + dz1 + 4) % 4) * 2 + (x_hi + p1) % 2
        return t0 + x_lo * (t1 - t0), c0 + x_lo * (c1 - c0)

    def piece_copy(g):
        t, c = where_from(g)
        spot = (y // 2) * 8 + 2 * c + y % 2
        return t, (
            pltpu.make_async_copy(pieces.at[g], placed.at[spot], out_r),
            remote(pieces.at[g], placed.at[spot], out_s.at[g], out_r, (t, col)),
        )

    def give(g, student):
        t, c = where_from(g)
        pieces[g] = student.astype(BF16)
        grads[y, x_lo, g] = ((student - targets[t, c].astype(F32)) * factor).astype(BF16)

    def place(g):
        t, (here, there) = piece_copy(g)

        @pl.when(t == row)
        def _():
            here.start()

        @pl.when(t != row)
        def _():
            there.start()

    def stage_c(s):
        swap_copy(s).wait_recv()
        first, count = STEPS[s]
        for g in range(first, first + count):
            give(g, over_y(x_lo, g) + got_x[g].astype(F32))
        for copy in grad_copies(s):
            copy.start()
        for g in range(first, first + count):
            place(g)

    def stage_d(s):
        grad_copies(s)[3].wait_recv()
        for copy in forward_copies(s):
            copy.start()

    def gradients(first, count):
        pieces_of = [grads[m % 4, m // 4, g] for g in range(first, first + count) for m in range(8)]
        return jnp.concatenate(pieces_of, axis=0).T

    def wait_gradients(s):
        if s == steps - 1:
            arrived_bytes(got_last, last_r.at[1])
        else:
            arrived_bytes(got_y.at[:, :, pl.ds(*STEPS[s])], grad_y_r.at[s])

    def stage_e(s, *more):
        for t in (s, *more):
            wait_gradients(t)
        first, count = STEPS[s]
        if s == 0:
            total[...] = jnp.dot(
                gradients(first, count), tokens_of(first, count, slice(None)), preferred_element_type=F32
            )
            return

        @pl.loop(0, 1 + len(more))
        def _(i):
            g = first + i * count
            pieces_of = [grads[m % 4, m // 4, g + k] for k in range(count) for m in range(8)]
            tokens = held[pl.ds(4 * g, 4 * count)].reshape(4 * CHUNK * count, depth)
            total[...] += jnp.dot(
                jnp.concatenate(pieces_of, axis=0).T, tokens, preferred_element_type=F32
            )

    def finish():
        for s in (steps - 2, steps - 1):
            wait_gradients(s)
        first = STEPS[steps - 2][0]
        count = len(GROUPS) - first
        g_t = gradients(first, count)
        span = depth // 4
        for i in range(4):
            ff = slice(i * span, (i + 1) * span)
            part = jnp.dot(g_t, tokens_of(first, count, ff), preferred_element_type=F32)
            grad[:, ff] = ((total[:, ff] + part) * keep[:, ff].astype(F32)).astype(BF16)
        arrived_bytes(placed, out_r)
        student_out[...] = placed[...].reshape(16 * PIECE, width).T

    stages = {"a": stage_a, "b": stage_b, "c": stage_c, "d": stage_d, "e": stage_e}

    start_tick(0)
    start_side(0)
    load_teacher.wait()
    for i in range(16):
        spread[i] = whole[:, i * width : (i + 1) * width]
    for copy in t_cols:
        copy.start()
    t_own.start()
    for c in range(4):
        across[c].start()

    for tick in range(11):
        if tick:
            arrived = [ups[tick - 1], downs[tick - 1]]
            names = [SEND_UP[tick - 1][1], SEND_DOWN[tick - 1][1]]
            for i, at in enumerate(ARRIVE_SIDE):
                if at == tick:
                    arrived.append(sides[i])
                    names.append(SEND_SIDE[i][1])
            for copy, name in zip(arrived, names):
                copy.wait_recv()
                across[NUMBER[name]].start()
            start_tick(tick)
        for what in PLAN[tick]:
            if what == "x":
                start_side(tick)
            elif what == "rows":
                t_own.wait()
                arrived_bytes(cols.at[pl.ds(0, 15)], teacher_r.at[0])
                for copy in t_rows:
                    copy.start()
                targets[row] = cols[pl.ds(y * 4, 4)]
            elif what == "targets":
                arrived_bytes(targets.at[pl.ds(0, 7)], teacher_r.at[1])
            elif what == "q":
                quantize()
                for copy in own:
                    copy.wait()
            elif what == "r":
                last_sum()
            elif what == "f":
                finish()
            else:
                stages[what[0]](*map(int, what[1:]))

    for g in range(16):
        t, (here, there) = piece_copy(g)

        @pl.when(t != row)
        def _():
            there.wait_send()

    sums = len(GROUPS) - 1
    for i, ref in enumerate((
        held.at[pl.ds(0, len(SEND_UP) + len(SEND_DOWN) + len(SEND_SIDE) + len(ARRIVALS))],
        got_y.at[:, :, pl.ds(0, sums)],
        swap.at[pl.ds(0, sums)],
        got_y.at[:, :, pl.ds(0, sums)],
        swap.at[pl.ds(0, sums)],
        swap.at[pl.ds(0, 14)],
        cols.at[pl.ds(0, 15)],
        targets.at[pl.ds(0, 7)],
    )):
        arrived_bytes(ref, sent.at[i])


def copy_out(student, grad, student_out, grad_out, sem):
    rows = grad.shape[0] // 6
    copies = [pltpu.make_async_copy(student, student_out, sem.at[6])]
    for i in range(6):
        part = pl.ds(i * rows, rows)
        copies.append(pltpu.make_async_copy(grad.at[part], grad_out.at[part], sem.at[i]))
    for copy in copies:
        copy.start()
    for copy in copies:
        copy.wait()


def local(hidden, weight, scale_exp, teacher):
    block, depth = hidden.shape
    width = weight.shape[1]
    tokens = block * lax.axis_size("col")
    groups, steps = len(GROUPS), len(STEPS)
    hidden = hidden.reshape(block // CHUNK, CHUNK, depth)
    dma = pltpu.SemaphoreType.DMA
    anywhere = pl.BlockSpec(memory_space=pl.ANY)
    student_out, grad = pl.pallas_call(
        functools.partial(kernel, 1.0 / math.sqrt(tokens)),
        out_shape=(
            pltpu.VMEM((width, 16 * PIECE), BF16),
            pltpu.VMEM((width, depth), BF16),
        ),
        in_specs=[anywhere, anywhere, pl.BlockSpec(memory_space=pltpu.SMEM), anywhere],
        out_specs=(pl.BlockSpec(memory_space=pltpu.VMEM),) * 2,
        scratch_shapes=[
            pltpu.VMEM((4 * groups, CHUNK, depth), BF16),
            pltpu.VMEM((width, depth), BF16),
            pltpu.VMEM((width, depth), BF16),
            pltpu.VMEM((width, depth), F32),
            pltpu.VMEM((16, depth), BF16),
            pltpu.VMEM((16, PIECE, width), BF16),
            pltpu.VMEM((4, 2, groups, PIECE, width), BF16),
            pltpu.VMEM((3, 2, groups, PIECE, width), BF16),
            pltpu.VMEM((groups, PIECE, width), BF16),
            pltpu.VMEM((groups, PIECE, width), BF16),
            pltpu.VMEM((7, PIECE, width), BF16),
            pltpu.VMEM((4, 2, groups, PIECE, width), BF16),
            pltpu.VMEM((groups, PIECE, width), BF16),
            pltpu.VMEM((16, PIECE, width), BF16),
            pltpu.VMEM((16, PIECE, width), BF16),
            pltpu.VMEM((8, 4, PIECE, width), BF16),
            dma((6,)), dma((8,)), dma((10,)), dma((10,)), dma((8,)), dma((steps,)),
            dma((steps,)), dma((steps,)), dma((steps,)), dma((steps,)), dma((groups,)), dma, dma((2,)), dma((2,)),
        ],
        compiler_params=pltpu.CompilerParams(
            collective_id=0, has_side_effects=True, vmem_limit_bytes=60 * 2**20
        ),
        cost_estimate=pl.CostEstimate(
            flops=4 * tokens * depth * width, bytes_accessed=3 * depth * width, transcendentals=0
        ),
    )(hidden, weight.T, scale_exp.T, teacher)
    student_out, grad = pl.pallas_call(
        copy_out,
        out_shape=tuple(jax.ShapeDtypeStruct(a.shape, a.dtype) for a in (student_out, grad)),
        in_specs=[pl.BlockSpec(memory_space=pltpu.VMEM)] * 2,
        out_specs=(anywhere, anywhere),
        scratch_shapes=[dma((7,))],
        compiler_params=pltpu.CompilerParams(vmem_limit_bytes=8 * 2**20),
    )(student_out, grad)
    return (student_out.T, grad.T)


def solution(mesh):
    placed = (P("col", "row"), P("row", "col"), P("row", "col"), P(("row", "col"), None))
    return jax.shard_map(
        local,
        mesh=mesh,
        in_specs=placed,
        out_specs=(P("row", "col"), P("row", "col")),
        check_vma=False,
    )
```

time: 118 us -> 103 us (0.87)
  Pallas kernels: 111 us -> 101 us
  local copies, waits for them, and re-layouts: 5 us -> 0 us
    pallas_call x1, Pallas kernels: 111 us -> 99.6 us  [local(): pl.pallas_call(functools.partial(kernel, 1.0 / math.sqrt(tokens)), out_sh...]
    unnamed x2 -> x0, local copies, waits for them, and re-layouts: 5 us -> none
    pallas_call x0 -> x1, Pallas kernels: none -> 1.6 us  [local(): pl.pallas_call(copy_out, out_shape=tuple((jax.ShapeDtypeStruct(a.shape, a...]
where the time goes in v3:
time: 103 us; the launch traced here: 102 us
  Pallas kernels  101 us (98%)
    pallas_call x1, Pallas kernels, local(): pl.pallas_call(functools.partial(kernel, 1.0 / math.sqrt(tokens)), out_sh...  99.6 us

profile of v3, /device:TPU:0, one launch (start us, length us, event | category | flops | bytes accessed | tf_op | source)
XLA Modules:
  0.0 102.0 jit_solution(6958110253999152369)
XLA Ops:
  0.6 99.6 %shard_map.59 = (bf16[288,256]{1,0:T(8,128)(2,1)S(1)}, bf16[288,4608]{1,0:T(8,128)(2,1)S(1)}) custom-call(bf16[4,32,4608]{2,1,0:T(8,128)(2,1)} %bitcast.7, bf16[288,4608]{1,0:T(8,128)(2,1)} %bitcast.5, s32[3,48]{1,0:T(4,128)} %bitcast.9, bf16[16,4608]{1,0:T(8,128)(2,1)} %teacher.1), custom_call_target="tpu_custom_call" | custom-call | flops 10871635968 | bytes 3981312 | tf_op jit(solution)/shard_map/pallas_call | solution.py:484
  100.2 1.6 %shard_map.60 = (bf16[288,256]{1,0:T(8,128)(2,1)}, bf16[288,4608]{1,0:T(8,128)(2,1)}) custom-call(bf16[288,256]{1,0:T(8,128)(2,1)S(1)} %get-tuple-element.6.student, bf16[288,4608]{1,0:T(8,128)(2,1)S(1)} %get-tuple-element.7.grad), custom_call_target="tpu_custom_call" | custom-call | tf_op jit(solution)/shard_map/pallas_call | solution.py:519

commit v4 on v3

--- a/solution.py
+++ b/solution.py
@@ -35,7 +35,9 @@
     ((*SIDE_DOWN, 3), (*SIDE_UP, 3)),
 )
 PLACE = {chunk: 4 * g + 2 * j for g, pair in enumerate(GROUPS) for j, chunk in enumerate(pair)}
-STEPS = ((0, 2), (2, 2), (4, 2), (6, 2), (8, 2), (10, 2), (12, 2), (14, 1), (15, 1))
+STEPS = ((0, 2), (2, 2), (4, 2), (6, 2), (8, 2), (10, 2), (12, 3), (15, 1))
+DIRECT = 6
+LATE = STEPS[DIRECT][0]
 SEND_UP = [
     ((*OWN, 0), (*DOWN, 0)),
     ((*OWN, 1), (*DOWN, 1)),
@@ -57,8 +59,8 @@
 ]
 START_UP = (0, 0, 1, 2, 3, 4, 5, 6, 7, 8)
 START_DOWN = (0, 0, 1, 2, 3, 4, 5, 6, 7, 8)
-START_SIDE = (0, 1, 2, 3, 4, 5, 6, 7)
-ARRIVE_SIDE = (2, 3, 4, 5, 6, 7, 8, 9)
+START_SIDE = (-1, 0, 1, 2, 3, 4, 5, 6)
+ARRIVE_SIDE = (2, 3, 4, 5, 6, 7, 8)
 ARRIVALS = (
     [(*OWN, c) for c in range(4)]
     + [there for _, there in SEND_UP]
@@ -67,17 +69,17 @@
 )
 NUMBER = {chunk: i for i, chunk in enumerate(ARRIVALS)}
 PLAN = (
-    ("q", "a0",),
+    ("q", "a0", "x",),
     ("x",),
     ("rows", "b0", "x", "a1",),
     ("x",),
     ("targets", "c0", "b1", "x",),
-    ("d0", "c1", "x", "a3", "a2",),
-    ("d1", "x", "a4", "e0",),
-    ("b3", "b2", "x", "e1",),
-    ("c3", "c2", "b4", "a5",),
-    ("d3", "d2", "c4", "a7", "a6",),
-    ("d4", "b5", "a8", "b7", "b6", "e23", "c5", "c7", "c6", "r", "e4", "d5", "d7", "d6", "e56", "f",),
+    ("c1", "x", "a3", "a2",),
+    ("x", "a4", "b3", "b2",),
+    ("d0", "d1", "b4",),
+    ("e0", "e1", "a5",),
+    ("c3", "c2", "c4", "w", "b5", "d3", "d2", "a6", "c5", "d4",),
+    ("a7", "d5", "e23", "r6", "r7", "e45", "f",),
 )
 
 
@@ -85,16 +87,22 @@
     factor,
     hidden, weight, scale, teacher,
     student_out, grad,
-    held, keep, quant, total, whole, spread, parts, got_y, swap, got_x, got_last, grads, pieces, placed, cols, targets,
-    load, sent, up_r, down_r, side_r, core_r, part_r, swap_r, grad_y_r, grad_x_r, out_s, out_r, last_r, teacher_r,
+    held, keep, quant, total, whole, spread, parts, got_y, swap, got_x, got_late, grads, pieces, placed, cols, targets,
+    load, sent, up_r, down_r, side_r, core_r, part_r, swap_r, grad_y_r, grad_x_r, out_s, out_r, late_r, teacher_r,
 ):
     row, col = lax.axis_index("row"), lax.axis_index("col")
     x_lo, y = row // 4, row % 4
     z, x_hi, core = col // 4, (col // 2) % 2, col % 2
-    width = parts.shape[-1]
+    width = grad.shape[0]
     depth = held.shape[-1]
     steps = len(STEPS)
-    last = STEPS[-1][0]
+
+    def piece(value):
+        return value[..., :width].astype(F32)
+
+    def padded(value):
+        spare = parts.shape[-1] - width
+        return jnp.concatenate([value, jnp.zeros((value.shape[0], spare), F32)], axis=1).astype(BF16)
 
     def in_col(dz, p, dc):
         return (row, ((z + dz + 4) % 4) * 4 + ((x_hi + p) % 2) * 2 + (core + dc) % 2)
@@ -110,6 +118,8 @@
     up, down, side, sibling = in_col(1, 0, 0), in_col(-1, 0, 0), in_col(0, 1, 0), in_col(0, 0, 1)
     partner = in_row(1, 0)
 
+    load_teacher = pltpu.make_async_copy(teacher, whole, load.at[5])
+    load_teacher.start()
     barrier = pltpu.get_barrier_semaphore()
     for k in range(1, 16):
         pl.semaphore_signal(barrier, inc=1, device_id=(row, (col + k) % 16), device_id_type=MESH)
@@ -126,8 +136,9 @@
         own[c].start()
     load_weight = pltpu.make_async_copy(weight, keep, load.at[4])
     load_weight.start()
-    load_teacher = pltpu.make_async_copy(teacher, whole, load.at[5])
-    load_teacher.start()
+    load_teacher.wait()
+    for i in range(16):
+        spread[i] = padded(whole[:, i * width : (i + 1) * width].astype(F32))
     pl.semaphore_wait(barrier, 22)
 
     def chunks_of(step):
@@ -254,55 +265,64 @@
         part = lax.dot_general(
             quant[...], tokens_of(first, count, slice(None)), (((1,), (1,)), ((), ())),
             preferred_element_type=F32,
-        ).T.astype(BF16)
+        ).T
+        part = padded(part)
         for g in range(count):
             for m in range(8):
                 at = (g * 8 + m) * PIECE
                 parts[m % 4, m // 4, first + g] = part[at : at + PIECE]
 
-        for copy in last_parts() if s == steps - 1 else part_copies(s):
+        for copy in direct_parts(s) if s >= DIRECT else part_copies(s):
             copy.start()
 
-    def last_parts():
+    def direct_parts(s):
+        first, count = STEPS[s]
         return [
             remote(
-                parts.at[(y + k % 4) % 4, (x_lo + k // 4) % 2, last],
-                got_last.at[k - 1],
+                parts.at[(y + k % 4) % 4, (x_lo + k // 4) % 2, pl.ds(first, count)],
+                got_late.at[k - 1, pl.ds(first - LATE, count)],
                 sent.at[5],
-                last_r.at[0],
+                late_r.at[0, s - DIRECT],
                 in_row(k // 4, k % 4),
             )
             for k in range(1, 8)
         ]
 
-    def last_grads():
-        mine = grads.at[y, x_lo, last]
+    def direct_grads(s):
+        mine = grads.at[y, x_lo, pl.ds(*STEPS[s])]
         return [
-            remote(mine, mine, sent.at[5], last_r.at[1], in_row(k // 4, k % 4))
+            remote(mine, mine, sent.at[8], late_r.at[1, s - DIRECT], in_row(k // 4, k % 4))
             for k in range(1, 8)
         ]
 
-    def last_sum():
-        arrived_bytes(got_last, last_r.at[0])
-        student = parts[y, x_lo, last].astype(F32)
-        for k in range(7):
-            student = student + got_last[k].astype(F32)
-        give(last, student)
-        for copy in last_grads():
+    def late_bytes(s):
+        first, count = STEPS[s]
+        return got_late.at[:, pl.ds(first - LATE, count)]
+
+    def stage_r(s):
+        arrived_bytes(late_bytes(s), late_r.at[0, s - DIRECT])
+        first, count = STEPS[s]
+        for g in range(first, first + count):
+            student = piece(parts[y, x_lo, g])
+            for k in range(7):
+                student = student + piece(got_late[k, g - LATE])
+            give(g, student)
+        for copy in direct_grads(s):
             copy.start()
-        place(last)
+        for g in range(first, first + count):
+            place(g)
 
     def over_y(x, g):
-        value = parts[y, x, g].astype(F32)
+        value = piece(parts[y, x, g])
         for k in range(3):
-            value = value + got_y[k, x, g].astype(F32)
+            value = value + piece(got_y[k, x, g])
         return value
 
     def stage_b(s):
         first, count = STEPS[s]
         arrived_bytes(got_y.at[:, :, pl.ds(first, count)], part_r.at[s])
         for g in range(first, first + count):
-            swap[g] = over_y(1 - x_lo, g).astype(BF16)
+            swap[g] = padded(over_y(1 - x_lo, g))
         swap_copy(s).start()
 
     def where_from(g):
@@ -321,8 +341,8 @@
 
     def give(g, student):
         t, c = where_from(g)
-        pieces[g] = student.astype(BF16)
-        grads[y, x_lo, g] = ((student - targets[t, c].astype(F32)) * factor).astype(BF16)
+        pieces[g] = padded(student)
+        grads[y, x_lo, g] = padded((student - piece(targets[t, c])) * factor)
 
     def place(g):
         t, (here, there) = piece_copy(g)
@@ -339,7 +359,7 @@
         swap_copy(s).wait_recv()
         first, count = STEPS[s]
         for g in range(first, first + count):
-            give(g, over_y(x_lo, g) + got_x[g].astype(F32))
+            give(g, over_y(x_lo, g) + piece(got_x[g]))
         for copy in grad_copies(s):
             copy.start()
         for g in range(first, first + count):
@@ -352,11 +372,11 @@
 
     def gradients(first, count):
         pieces_of = [grads[m % 4, m // 4, g] for g in range(first, first + count) for m in range(8)]
-        return jnp.concatenate(pieces_of, axis=0).T
+        return jnp.concatenate(pieces_of, axis=0)[:, :width].T
 
     def wait_gradients(s):
-        if s == steps - 1:
-            arrived_bytes(got_last, last_r.at[1])
+        if s >= DIRECT:
+            arrived_bytes(late_bytes(s), late_r.at[1, s - DIRECT])
         else:
             arrived_bytes(got_y.at[:, :, pl.ds(*STEPS[s])], grad_y_r.at[s])
 
@@ -376,7 +396,7 @@
             pieces_of = [grads[m % 4, m // 4, g + k] for k in range(count) for m in range(8)]
             tokens = held[pl.ds(4 * g, 4 * count)].reshape(4 * CHUNK * count, depth)
             total[...] += jnp.dot(
-                jnp.concatenate(pieces_of, axis=0).T, tokens, preferred_element_type=F32
+                jnp.concatenate(pieces_of, axis=0)[:, :width].T, tokens, preferred_element_type=F32
             )
 
     def finish():
@@ -391,17 +411,14 @@
             part = jnp.dot(g_t, tokens_of(first, count, ff), preferred_element_type=F32)
             grad[:, ff] = ((total[:, ff] + part) * keep[:, ff].astype(F32)).astype(BF16)
         arrived_bytes(placed, out_r)
-        student_out[...] = placed[...].reshape(16 * PIECE, width).T
-
-    stages = {"a": stage_a, "b": stage_b, "c": stage_c, "d": stage_d, "e": stage_e}
-
-    start_tick(0)
-    start_side(0)
-    load_teacher.wait()
-    for i in range(16):
-        spread[i] = whole[:, i * width : (i + 1) * width]
+        student_out[...] = placed[...].reshape(16 * PIECE, -1)[:, :width].T
+
+    stages = {"a": stage_a, "r": stage_r, "b": stage_b, "c": stage_c, "d": stage_d, "e": stage_e}
+
     for copy in t_cols:
         copy.start()
+    start_tick(0)
+    start_side(-1)
     t_own.start()
     for c in range(4):
         across[c].start()
@@ -421,6 +438,9 @@
         for what in PLAN[tick]:
             if what == "x":
                 start_side(tick)
+            elif what == "w":
+                sides[-1].wait_recv()
+                across[-1].start()
             elif what == "rows":
                 t_own.wait()
                 arrived_bytes(cols.at[pl.ds(0, 15)], teacher_r.at[0])
@@ -433,8 +453,6 @@
                 quantize()
                 for copy in own:
                     copy.wait()
-            elif what == "r":
-                last_sum()
             elif what == "f":
                 finish()
             else:
@@ -447,16 +465,17 @@
         def _():
             there.wait_send()
 
-    sums = len(GROUPS) - 1
+    sums = LATE
     for i, ref in enumerate((
         held.at[pl.ds(0, len(SEND_UP) + len(SEND_DOWN) + len(SEND_SIDE) + len(ARRIVALS))],
         got_y.at[:, :, pl.ds(0, sums)],
         swap.at[pl.ds(0, sums)],
         got_y.at[:, :, pl.ds(0, sums)],
         swap.at[pl.ds(0, sums)],
-        swap.at[pl.ds(0, 14)],
+        got_late,
         cols.at[pl.ds(0, 15)],
         targets.at[pl.ds(0, 7)],
+        got_late,
     )):
         arrived_bytes(ref, sent.at[i])
 
@@ -478,6 +497,7 @@
     width = weight.shape[1]
     tokens = block * lax.axis_size("col")
     groups, steps = len(GROUPS), len(STEPS)
+    wide = -(-width // 128) * 128
     hidden = hidden.reshape(block // CHUNK, CHUNK, depth)
     dma = pltpu.SemaphoreType.DMA
     anywhere = pl.BlockSpec(memory_space=pl.ANY)
@@ -495,19 +515,19 @@
             pltpu.VMEM((width, depth), BF16),
             pltpu.VMEM((width, depth), F32),
             pltpu.VMEM((16, depth), BF16),
-            pltpu.VMEM((16, PIECE, width), BF16),
-            pltpu.VMEM((4, 2, groups, PIECE, width), BF16),
-            pltpu.VMEM((3, 2, groups, PIECE, width), BF16),
-            pltpu.VMEM((groups, PIECE, width), BF16),
-            pltpu.VMEM((groups, PIECE, width), BF16),
-            pltpu.VMEM((7, PIECE, width), BF16),
-            pltpu.VMEM((4, 2, groups, PIECE, width), BF16),
-            pltpu.VMEM((groups, PIECE, width), BF16),
-            pltpu.VMEM((16, PIECE, width), BF16),
-            pltpu.VMEM((16, PIECE, width), BF16),
-            pltpu.VMEM((8, 4, PIECE, width), BF16),
-            dma((6,)), dma((8,)), dma((10,)), dma((10,)), dma((8,)), dma((steps,)),
-            dma((steps,)), dma((steps,)), dma((steps,)), dma((steps,)), dma((groups,)), dma, dma((2,)), dma((2,)),
+            pltpu.VMEM((16, PIECE, wide), BF16),
+            pltpu.VMEM((4, 2, groups, PIECE, wide), BF16),
+            pltpu.VMEM((3, 2, groups, PIECE, wide), BF16),
+            pltpu.VMEM((groups, PIECE, wide), BF16),
+            pltpu.VMEM((groups, PIECE, wide), BF16),
+            pltpu.VMEM((7, groups - LATE, PIECE, wide), BF16),
+            pltpu.VMEM((4, 2, groups, PIECE, wide), BF16),
+            pltpu.VMEM((groups, PIECE, wide), BF16),
+            pltpu.VMEM((16, PIECE, wide), BF16),
+            pltpu.VMEM((16, PIECE, wide), BF16),
+            pltpu.VMEM((8, 4, PIECE, wide), BF16),
+            dma((6,)), dma((9,)), dma((10,)), dma((10,)), dma((8,)), dma((steps,)),
+            dma((steps,)), dma((steps,)), dma((steps,)), dma((steps,)), dma((groups,)), dma, dma((2, steps - DIRECT)), dma((2,)),
         ],
         compiler_params=pltpu.CompilerParams(
             collective_id=0, has_side_effects=True, vmem_limit_bytes=60 * 2**20

time: 103 us -> 99.2 us (0.963)
  Pallas kernels: 101 us -> 97.6 us
    pallas_call x1, Pallas kernels: 99.6 us -> 96 us  [local(): pl.pallas_call(functools.partial(kernel, 1.0 / math.sqrt(tokens)), out_sh...]
where the time goes in v4:
time: 99.2 us; the launch traced here: 98.4 us
  Pallas kernels  97.6 us (98%)
    pallas_call x1, Pallas kernels, local(): pl.pallas_call(functools.partial(kernel, 1.0 / math.sqrt(tokens)), out_sh...  96 us

profile of v4, /device:TPU:0, one launch (start us, length us, event | category | flops | bytes accessed | tf_op | source)
XLA Modules:
  0.0 98.4 jit_solution(17969770797236826928)
XLA Ops:
  0.6 96.0 %shard_map.59 = (bf16[288,256]{1,0:T(8,128)(2,1)S(1)}, bf16[288,4608]{1,0:T(8,128)(2,1)S(1)}) custom-call(bf16[4,32,4608]{2,1,0:T(8,128)(2,1)} %bitcast.7, bf16[288,4608]{1,0:T(8,128)(2,1)} %bitcast.5, s32[3,48]{1,0:T(4,128)} %bitcast.9, bf16[16,4608]{1,0:T(8,128)(2,1)} %teacher.1), custom_call_target="tpu_custom_call" | custom-call | flops 10871635968 | bytes 3981312 | tf_op jit(solution)/shard_map/pallas_call | solution.py:504
  96.6 1.6 %shard_map.60 = (bf16[288,256]{1,0:T(8,128)(2,1)}, bf16[288,4608]{1,0:T(8,128)(2,1)}) custom-call(bf16[288,256]{1,0:T(8,128)(2,1)S(1)} %get-tuple-element.6.student, bf16[288,4608]{1,0:T(8,128)(2,1)S(1)} %get-tuple-element.7.grad), custom_call_target="tpu_custom_call" | custom-call | tf_op jit(solution)/shard_map/pallas_call | solution.py:539

commit v5 on v4

--- a/solution.py
+++ b/solution.py
@@ -36,7 +36,7 @@
 )
 PLACE = {chunk: 4 * g + 2 * j for g, pair in enumerate(GROUPS) for j, chunk in enumerate(pair)}
 STEPS = ((0, 2), (2, 2), (4, 2), (6, 2), (8, 2), (10, 2), (12, 3), (15, 1))
-DIRECT = 6
+DIRECT = 7
 LATE = STEPS[DIRECT][0]
 SEND_UP = [
     ((*OWN, 0), (*DOWN, 0)),
@@ -75,11 +75,11 @@
     ("x",),
     ("targets", "c0", "b1", "x",),
     ("c1", "x", "a3", "a2",),
-    ("x", "a4", "b3", "b2",),
+    ("a4", "b3", "b2", "x",),
     ("d0", "d1", "b4",),
-    ("e0", "e1", "a5",),
-    ("c3", "c2", "c4", "w", "b5", "d3", "d2", "a6", "c5", "d4",),
-    ("a7", "d5", "e23", "r6", "r7", "e45", "f",),
+    ("c3", "c2", "e0", "a5", "e1",),
+    ("c4", "d3", "d2", "w", "a6", "b5", "d4",),
+    ("a7", "c5", "b6", "d5", "c6", "r7", "e23", "d6", "e45", "f",),
 )
 
 
@@ -98,11 +98,10 @@
     steps = len(STEPS)
 
     def piece(value):
-        return value[..., :width].astype(F32)
-
-    def padded(value):
-        spare = parts.shape[-1] - width
-        return jnp.concatenate([value, jnp.zeros((value.shape[0], spare), F32)], axis=1).astype(BF16)
+        return value.astype(F32)
+
+    def rounded(value):
+        return value.astype(BF16)
 
     def in_col(dz, p, dc):
         return (row, ((z + dz + 4) % 4) * 4 + ((x_hi + p) % 2) * 2 + (core + dc) % 2)
@@ -138,7 +137,7 @@
     load_weight.start()
     load_teacher.wait()
     for i in range(16):
-        spread[i] = padded(whole[:, i * width : (i + 1) * width].astype(F32))
+        spread[i] = whole[:, i * width : (i + 1) * width]
     pl.semaphore_wait(barrier, 22)
 
     def chunks_of(step):
@@ -266,7 +265,7 @@
             quant[...], tokens_of(first, count, slice(None)), (((1,), (1,)), ((), ())),
             preferred_element_type=F32,
         ).T
-        part = padded(part)
+        part = rounded(part)
         for g in range(count):
             for m in range(8):
                 at = (g * 8 + m) * PIECE
@@ -322,7 +321,7 @@
         first, count = STEPS[s]
         arrived_bytes(got_y.at[:, :, pl.ds(first, count)], part_r.at[s])
         for g in range(first, first + count):
-            swap[g] = padded(over_y(1 - x_lo, g))
+            swap[g] = rounded(over_y(1 - x_lo, g))
         swap_copy(s).start()
 
     def where_from(g):
@@ -341,8 +340,8 @@
 
     def give(g, student):
         t, c = where_from(g)
-        pieces[g] = padded(student)
-        grads[y, x_lo, g] = padded((student - piece(targets[t, c])) * factor)
+        pieces[g] = rounded(student)
+        grads[y, x_lo, g] = rounded((student - piece(targets[t, c])) * factor)
 
     def place(g):
         t, (here, there) = piece_copy(g)
@@ -372,7 +371,7 @@
 
     def gradients(first, count):
         pieces_of = [grads[m % 4, m // 4, g] for g in range(first, first + count) for m in range(8)]
-        return jnp.concatenate(pieces_of, axis=0)[:, :width].T
+        return jnp.concatenate(pieces_of, axis=0).T
 
     def wait_gradients(s):
         if s >= DIRECT:
@@ -396,7 +395,7 @@
             pieces_of = [grads[m % 4, m // 4, g + k] for k in range(count) for m in range(8)]
             tokens = held[pl.ds(4 * g, 4 * count)].reshape(4 * CHUNK * count, depth)
             total[...] += jnp.dot(
-                jnp.concatenate(pieces_of, axis=0)[:, :width].T, tokens, preferred_element_type=F32
+                jnp.concatenate(pieces_of, axis=0).T, tokens, preferred_element_type=F32
             )
 
     def finish():
@@ -411,7 +410,7 @@
             part = jnp.dot(g_t, tokens_of(first, count, ff), preferred_element_type=F32)
             grad[:, ff] = ((total[:, ff] + part) * keep[:, ff].astype(F32)).astype(BF16)
         arrived_bytes(placed, out_r)
-        student_out[...] = placed[...].reshape(16 * PIECE, -1)[:, :width].T
+        student_out[...] = placed[...].reshape(16 * PIECE, width).T
 
     stages = {"a": stage_a, "r": stage_r, "b": stage_b, "c": stage_c, "d": stage_d, "e": stage_e}
 
@@ -497,7 +496,6 @@
     width = weight.shape[1]
     tokens = block * lax.axis_size("col")
     groups, steps = len(GROUPS), len(STEPS)
-    wide = -(-width // 128) * 128
     hidden = hidden.reshape(block // CHUNK, CHUNK, depth)
     dma = pltpu.SemaphoreType.DMA
     anywhere = pl.BlockSpec(memory_space=pl.ANY)
@@ -515,17 +513,17 @@
             pltpu.VMEM((width, depth), BF16),
             pltpu.VMEM((width, depth), F32),
             pltpu.VMEM((16, depth), BF16),
-            pltpu.VMEM((16, PIECE, wide), BF16),
-            pltpu.VMEM((4, 2, groups, PIECE, wide), BF16),
-            pltpu.VMEM((3, 2, groups, PIECE, wide), BF16),
-            pltpu.VMEM((groups, PIECE, wide), BF16),
-            pltpu.VMEM((groups, PIECE, wide), BF16),
-            pltpu.VMEM((7, groups - LATE, PIECE, wide), BF16),
-            pltpu.VMEM((4, 2, groups, PIECE, wide), BF16),
-            pltpu.VMEM((groups, PIECE, wide), BF16),
-            pltpu.VMEM((16, PIECE, wide), BF16),
-            pltpu.VMEM((16, PIECE, wide), BF16),
-            pltpu.VMEM((8, 4, PIECE, wide), BF16),
+            pltpu.VMEM((16, PIECE, width), BF16),
+            pltpu.VMEM((4, 2, groups, PIECE, width), BF16),
+            pltpu.VMEM((3, 2, groups, PIECE, width), BF16),
+            pltpu.VMEM((groups, PIECE, width), BF16),
+            pltpu.VMEM((groups, PIECE, width), BF16),
+            pltpu.VMEM((7, groups - LATE, PIECE, width), BF16),
+            pltpu.VMEM((4, 2, groups, PIECE, width), BF16),
+            pltpu.VMEM((groups, PIECE, width), BF16),
+            pltpu.VMEM((16, PIECE, width), BF16),
+            pltpu.VMEM((16, PIECE, width), BF16),
+            pltpu.VMEM((8, 4, PIECE, width), BF16),
             dma((6,)), dma((9,)), dma((10,)), dma((10,)), dma((8,)), dma((steps,)),
             dma((steps,)), dma((steps,)), dma((steps,)), dma((steps,)), dma((groups,)), dma, dma((2, steps - DIRECT)), dma((2,)),
         ],

time: 99.2 us -> 97.7 us (0.985)
  Pallas kernels: 97.6 us -> 96.6 us
    pallas_call x1, Pallas kernels: 96 us -> 95 us  [local(): pl.pallas_call(functools.partial(kernel, 1.0 / math.sqrt(tokens)), out_sh...]
where the time goes in v5:
time: 97.7 us; the launch traced here: 97.4 us
  Pallas kernels  96.6 us (99%)
    pallas_call x1, Pallas kernels, local(): pl.pallas_call(functools.partial(kernel, 1.0 / math.sqrt(tokens)), out_sh...  95 us

profile of v5, /device:TPU:0, one launch (start us, length us, event | category | flops | bytes accessed | tf_op | source)
XLA Modules:
  0.0 97.4 jit_solution(10801669462693893311)
XLA Ops:
  0.6 95.0 %shard_map.59 = (bf16[288,256]{1,0:T(8,128)(2,1)S(1)}, bf16[288,4608]{1,0:T(8,128)(2,1)S(1)}) custom-call(bf16[4,32,4608]{2,1,0:T(8,128)(2,1)} %bitcast.7, bf16[288,4608]{1,0:T(8,128)(2,1)} %bitcast.5, s32[3,48]{1,0:T(4,128)} %bitcast.9, bf16[16,4608]{1,0:T(8,128)(2,1)} %teacher.1), custom_call_target="tpu_custom_call" | custom-call | flops 10871635968 | bytes 3981312 | tf_op jit(solution)/shard_map/pallas_call | solution.py:502
  95.6 1.6 %shard_map.60 = (bf16[288,256]{1,0:T(8,128)(2,1)}, bf16[288,4608]{1,0:T(8,128)(2,1)}) custom-call(bf16[288,256]{1,0:T(8,128)(2,1)S(1)} %get-tuple-element.6.student, bf16[288,4608]{1,0:T(8,128)(2,1)S(1)} %get-tuple-element.7.grad), custom_call_target="tpu_custom_call" | custom-call | tf_op jit(solution)/shard_map/pallas_call | solution.py:537
